TPU v7x, 32 devices: a whole 2x2x4 slice. The times are simulated.
32 devices in a mesh: seq: 8 (over z, y), head: 4 (over x, core).
Axes of the slice: x: 2, y: 2, z: 4, core: 2. Of those that a mesh axis runs over, the one named last changes fastest.
Arguments:
- x_in: bfloat16 [2, 2048, 2048], P(None, ('seq', 'head')), may hold values from -6 to 6
- lengths: int32 [2, 3], replicated, may hold values from 128 to 1792, as said below
- cotangent: bfloat16 [2, 2048, 2048], P(None, ('seq', 'head')), may hold values from -6 to 6
- w_in: float32 [2048, 8512], P(('seq', 'head')), may hold values from -0.125 to 0.125
- m_in: float32 [2048, 8512], P(('seq', 'head')), may hold values from -112 to 112
- v_in: float32 [2048, 8512], P(('seq', 'head')), may hold values from 163.84 to 655.36
- w_out: float32 [4096, 2048], P(('seq', 'head')), may hold values from -0.09375 to 0.09375
- m_out: float32 [4096, 2048], P(('seq', 'head')), may hold values from -384 to 384
- v_out: float32 [4096, 2048], P(('seq', 'head')), may hold values from 1761.28 to 6963.2
- conv_w: float32 [4352, 4], P(('seq', 'head')), may hold values from -3 to 3
- m_conv: float32 [4352, 4], P(('seq', 'head')), may hold values from -112 to 112
- v_conv: float32 [4352, 4], P(('seq', 'head')), may hold values from 163.84 to 655.36
- vectors: float32 [10496], P(('seq', 'head')), may hold values from -0.9 to 1.7
- m_vec: float32 [10496], P(('seq', 'head')), may hold values from -256 to 256
- v_vec: float32 [10496], P(('seq', 'head')), may hold values from 819.2 to 3481.6
- head_params: float32 [3, 64], P(None, 'head'), may hold values from -13.2 to 8
- m_head: float32 [3, 64], P(None, 'head'), may hold values from -768 to 768
- v_head: float32 [3, 64], P(None, 'head'), may hold values from 6963.2 to 28672
Outputs:
- layer_out: bfloat16 [2, 2048, 2048], P(None, ('seq', 'head'))
- input_grad: bfloat16 [2, 2048, 2048], P(None, ('seq', 'head'))
- w_in_new: float32 [2048, 8512], P(('seq', 'head'))
- m_in_new: float32 [2048, 8512], P(('seq', 'head'))
- v_in_new: float32 [2048, 8512], P(('seq', 'head'))
- w_out_new: float32 [4096, 2048], P(('seq', 'head'))
- m_out_new: float32 [4096, 2048], P(('seq', 'head'))
- v_out_new: float32 [4096, 2048], P(('seq', 'head'))
- conv_new: float32 [4352, 4], P(('seq', 'head'))
- m_conv_new: float32 [4352, 4], P(('seq', 'head'))
- v_conv_new: float32 [4352, 4], P(('seq', 'head'))
- vec_new: float32 [10496], P(('seq', 'head'))
- m_vec_new: float32 [10496], P(('seq', 'head'))
- v_vec_new: float32 [10496], P(('seq', 'head'))
- head_new: float32 [3, 64], P(None, 'head')
- m_head_new: float32 [3, 64], P(None, 'head')
- v_head_new: float32 [3, 64], P(None, 'head')
Inputs may be any that keep to these rules, and one draw needn't show every extreme that they name: In each group the first and the last sequence hold at least 128 and fewer than 256 tokens, the middle one the rest; a group's lengths sum to 2048; in one group both the first and the last hold exactly 128.
All inputs are finite; a program needn't handle non-finite values.
Results may differ from a plain program's by a relative error of at most 0.01.
The roundings to bfloat16 on the way count: a program that leaves them out, or rounds other values in their place, can miss the bound.
Values may be sent and summed in bfloat16 or wider, within the bound.
No kernel may reach another device: no remote copies, remote signals or barrier semaphores. Data moves between devices by JAX's collectives and lax.ppermute only.
A program may use at most 384 MiB of HBM per device.

v0:
```python
import jax
import jax.numpy as jnp
from jax import lax
from jax.sharding import PartitionSpec as P

D = 2048
HEADS = 64
HEAD_DIM = 64
STATE = 128
KW = 4
BLOCK = 256
STEP = 4
INNER = 4096
CONV = 4352


EPS = 1e-05
BETA_ONE = 0.5
BETA_TWO = 0.7
ADAM_EPS = 1e-08
DECAY = 0.1
rate_input = 0.02
rate_output = 0.015
rate_conv = 0.3
rate_vector = 0.5
rate_head = 0.5
HIGH = lax.Precision.HIGHEST


def passed_along(value, axis, by):
    peers = lax.axis_size(axis)
    pairs = [(i, i + by) for i in range(peers) if 0 <= i + by < peers]
    return lax.ppermute(value, axis, pairs)


def prefix(part, axis, combine, identity):
    place = lax.axis_index(axis)
    gathered = jax.tree.map(lambda a: lax.all_gather(a, axis), part)
    state = jax.tree.map(lambda a, e: jnp.zeros_like(a) + jnp.asarray(e, a.dtype), part, identity)

    def one(step, state):
        return combine(
            state, jax.tree.map(lambda a: lax.dynamic_index_in_dim(a, step, 0, False), gathered)
        )

    return lax.fori_loop(0, place, one, state)


def carried_in(value, axis, combine, identity):
    peers, position = (lax.axis_size(axis), lax.axis_index(axis))
    everything = jax.tree.map(
        lambda part, kind: lax.all_gather(part.astype(kind), axis),
        value,
        (jnp.bfloat16, jnp.bfloat16),
    )
    start = jax.tree.map(
        lambda part, zero: jnp.broadcast_to(jnp.asarray(zero, part.dtype), part.shape),
        value,
        identity,
    )

    def step(k, before):
        at = peers - 1 - k
        reached = at > position
        new = combine(
            before, jax.tree.map(lambda part, own: part[at].astype(own.dtype), everything, value)
        )
        return jax.tree.map(lambda a, b: jnp.where(reached, a, b), new, before)

    return lax.fori_loop(0, peers, step, start)


def start_flags(length_row, first_pos, count):
    offsets = jnp.cumsum(length_row) - length_row
    places = first_pos + jnp.arange(count)
    return jnp.any(places[:, None] == offsets[None, :], axis=1).astype(jnp.int32)


def conv_mix(extended, taps, shift_term, start_ext):
    tok_span = extended.shape[0] - (KW - 1)
    counts = jnp.cumsum(start_ext)
    total = shift_term[None, :] + taps[:, KW - 1][None, :] * extended[KW - 1 :]
    for tap in range(KW - 1):
        lag = KW - 1 - tap
        valid = counts[KW - 1 :] - counts[KW - 1 - lag : KW - 1 - lag + tok_span] == 0
        total = total + taps[:, tap][None, :] * extended[tap : tap + tok_span] * valid[
            :, None
        ].astype(extended.dtype)
    return total


def block_step(memory, block):
    values, key_rows, query_rows, step_size, log_decay, starts = block
    running = jnp.cumsum(log_decay, axis=0)
    segment = jnp.cumsum(starts)
    places = jnp.arange(starts.shape[0])
    within = (segment[:, None] == segment[None, :]) & (places[:, None] >= places[None, :])
    gaps = running[:, None, :] - running[None, :, :]
    decays = jnp.exp(jnp.where(within[:, :, None], gaps, 0.0)) * within[:, :, None].astype(
        log_decay.dtype
    )
    scores = jnp.dot(query_rows, key_rows.T, precision=HIGH)
    weighted = values * step_size[:, :, None]
    output_h = jnp.einsum("tsh,shp->thp", scores[:, :, None] * decays, weighted, precision=HIGH)
    inflow = jnp.exp(running) * (segment == 0).astype(log_decay.dtype)[:, None]
    output_h = (
        output_h
        + jnp.einsum("tn,hpn->thp", query_rows, memory, precision=HIGH) * inflow[:, :, None]
    )
    to_end = (
        jnp.exp(running[-1][None, :] - running)
        * (segment == segment[-1]).astype(log_decay.dtype)[:, None]
    )
    carried = jnp.exp(running[-1]) * (segment[-1] == 0).astype(log_decay.dtype)
    memory = carried[:, None, None] * memory + jnp.einsum(
        "sh,shp,sn->hpn", to_end, weighted, key_rows, precision=HIGH
    )
    return (memory, output_h)


def ssd_run(values, key_rows, query_rows, step_size, log_decay, starts):
    blocks = values.shape[0] // BLOCK

    def blocked(array):
        return array.reshape((blocks, BLOCK) + array.shape[1:])

    memory = jnp.zeros((values.shape[1], values.shape[2], key_rows.shape[1]), values.dtype)
    memory, outputs = lax.scan(
        jax.checkpoint(block_step),
        memory,
        (
            blocked(values),
            blocked(key_rows),
            blocked(query_rows),
            blocked(step_size),
            blocked(log_decay),
            blocked(starts),
        ),
    )
    return (outputs.reshape(values.shape), memory)


def local_scan(extended, step_raw, taps, shift_term, head_terms, start_ext):
    x_width = taps.shape[0] - 2 * STATE
    head_count = head_terms.shape[1]
    conv = jax.vmap(conv_mix, in_axes=(0, None, None, 0))(extended, taps, shift_term, start_ext)
    act = jax.nn.silu(conv)
    tok_span = act.shape[1]
    values = act[..., :x_width].reshape(act.shape[0], tok_span, head_count, HEAD_DIM)
    key_rows = act[..., x_width : x_width + STATE]
    query_rows = act[..., x_width + STATE :]
    step_size = jax.nn.softplus(step_raw + head_terms[0])
    log_decay = -jnp.exp(head_terms[1]) * step_size
    starts = start_ext[:, KW - 1 :]
    scanned, memory = jax.vmap(ssd_run)(values, key_rows, query_rows, step_size, log_decay, starts)
    scanned = scanned + head_terms[2][None, None, :, None] * values
    fresh = (jnp.cumsum(starts, axis=1) == 0).astype(jnp.float32)
    w_cum = jnp.exp(jnp.cumsum(log_decay, axis=1)) * fresh[..., None]
    return (scanned, memory, w_cum[:, -1], query_rows, w_cum)


def carry_join(earlier, later):
    return (earlier[0] * later[0], later[0][..., None, None] * earlier[1] + later[1])


def gate_norm(gate_in, scan_out, gate_gain):
    gated = scan_out * jax.nn.silu(gate_in)
    return gated * lax.rsqrt(jnp.mean(gated * gated, axis=-1, keepdims=True) + EPS) * gate_gain


def front_norm(x_float, norm_gain):
    return (
        x_float * lax.rsqrt(jnp.mean(x_float * x_float, axis=-1, keepdims=True) + EPS) * norm_gain
    )


def adam(weight, first, second, grad, rate):
    first_new = BETA_ONE * first + (1.0 - BETA_ONE) * grad
    second_new = BETA_TWO * second + (1.0 - BETA_TWO) * grad * grad
    update = (
        first_new
        / (1.0 - BETA_ONE**STEP)
        / (jnp.sqrt(second_new / (1.0 - BETA_TWO**STEP)) + ADAM_EPS)
    )
    return (weight - rate * (update + DECAY * weight), first_new, second_new)


def local(
    x_in,
    lengths,
    cotangent,
    w_in,
    m_in,
    v_in,
    w_out,
    m_out,
    v_out,
    conv_w,
    m_conv,
    v_conv,
    vectors,
    m_vec,
    v_vec,
    head_params,
    m_head,
    v_head,
):
    head_size = lax.axis_size("head")
    heads_dev = HEADS // head_size
    width_dev = heads_dev * HEAD_DIM
    group_count = x_in.shape[0]
    tok_span = x_in.shape[1] * head_size
    seq_place = lax.axis_index("seq")
    head_place = lax.axis_index("head")
    first_pos = seq_place * tok_span - (KW - 1)
    start_ext = jax.vmap(lambda length_row: start_flags(length_row, first_pos, tok_span + KW - 1))(
        lengths
    )
    gathered = (
        lax.all_gather(w_in.astype(jnp.bfloat16), ("seq", "head"), axis=0, tiled=True),
        lax.all_gather(w_out.astype(jnp.bfloat16), ("seq", "head"), axis=0, tiled=True),
        lax.all_gather(conv_w.astype(jnp.bfloat16), ("seq", "head"), axis=0, tiled=True),
        lax.all_gather(vectors.astype(jnp.bfloat16), ("seq", "head"), axis=0, tiled=True),
    )

    def forward(weights):
        w_in_b, w_out_b, taps_b, vec_b = weights
        vec_f = vec_b.astype(jnp.float32)
        norm_gain = vec_f[:D]
        conv_bias = vec_f[D : D + CONV]
        gate_gain = vec_f[D + CONV :]
        x_float = x_in.astype(jnp.float32)
        normed = front_norm(x_float, norm_gain).astype(jnp.bfloat16)
        proj = jnp.einsum("gtd,dk->gtk", normed, w_in_b, preferred_element_type=jnp.float32)
        gate_in = proj[..., :INNER]
        x_part = proj[..., INNER : 2 * INNER].astype(jnp.bfloat16)
        shared = proj[..., 2 * INNER : INNER + CONV].astype(jnp.bfloat16)
        step_low = proj[..., INNER + CONV :].astype(jnp.bfloat16)
        x_heads, step_heads = (
            lax.all_to_all(x_part, "head", split_axis=2, concat_axis=1, tiled=True),
            lax.all_to_all(step_low, "head", split_axis=2, concat_axis=1, tiled=True),
        )
        shared_all = lax.all_gather(shared, "head", axis=1, tiled=True)
        local_in = jnp.concatenate([x_heads, shared_all], axis=-1)
        rim_rows = passed_along(local_in[:, tok_span - (KW - 1) :], "seq", 1)
        extended = jnp.concatenate([rim_rows, local_in], axis=1).astype(jnp.float32)
        taps_local = jnp.concatenate(
            [
                lax.dynamic_slice_in_dim(taps_b, head_place * width_dev, width_dev, 0),
                taps_b[INNER:],
            ],
            axis=0,
        ).astype(jnp.float32)
        bias_local = jnp.concatenate(
            [
                lax.dynamic_slice_in_dim(conv_bias, head_place * width_dev, width_dev, 0),
                conv_bias[INNER:],
            ],
            axis=0,
        )
        step_float = step_heads.astype(jnp.float32)
        scanned, memory, carry_gate, query_rows, w_cum = local_scan(
            extended, step_float, taps_local, bias_local, head_params, start_ext
        )
        identity = (jnp.ones_like(carry_gate), jnp.zeros_like(memory))
        incoming = prefix((carry_gate, memory), "seq", carry_join, identity)[1]
        scanned = scanned + jnp.einsum(
            "gtn,ghpn,gth->gthp", query_rows, incoming, w_cum, precision=HIGH
        )
        scan_send = scanned.reshape(group_count, tok_span, width_dev).astype(jnp.bfloat16)
        scan_tok = lax.all_to_all(
            scan_send, "head", split_axis=1, concat_axis=2, tiled=True
        ).astype(jnp.float32)
        gnorm = gate_norm(gate_in, scan_tok, gate_gain).astype(jnp.bfloat16)
        branch = jnp.einsum("gti,id->gtd", gnorm, w_out_b, preferred_element_type=jnp.float32)
        result = (x_float + branch).astype(jnp.bfloat16)
        kept_values = (
            normed,
            gate_in,
            extended,
            step_float,
            taps_local,
            bias_local,
            incoming,
            query_rows,
            w_cum,
            carry_gate,
            scan_tok,
            gnorm,
            gate_gain,
            norm_gain,
            x_float,
        )
        return (result, kept_values)

    result, kept = forward(gathered)
    weights_back = (
        lax.all_gather(w_in.astype(jnp.bfloat16), ("seq", "head"), axis=0, tiled=True),
        lax.all_gather(w_out.astype(jnp.bfloat16), ("seq", "head"), axis=0, tiled=True),
        lax.all_gather(conv_w.astype(jnp.bfloat16), ("seq", "head"), axis=0, tiled=True),
        lax.all_gather(vectors.astype(jnp.bfloat16), ("seq", "head"), axis=0, tiled=True),
    )
    unused, kept = forward(weights_back)
    (
        normed,
        gate_in,
        extended,
        step_float,
        taps_local,
        bias_local,
        incoming,
        query_rows,
        w_cum,
        carry_gate,
        scan_tok,
        gnorm,
        gate_gain,
        norm_gain,
        x_float,
    ) = kept
    w_in_b = weights_back[0]
    w_out_b = weights_back[1]
    back_float = cotangent.astype(jnp.float32)
    grad_out = jnp.einsum("gti,gtd->id", gnorm, cotangent, preferred_element_type=jnp.float32)
    grad_gnorm = jnp.einsum("gtd,id->gti", cotangent, w_out_b, preferred_element_type=jnp.float32)
    unused_gate, pull_gate = jax.vjp(gate_norm, gate_in, scan_tok, gate_gain)
    grad_gate_in, grad_scan_tok, grad_gate_gain = pull_gate(grad_gnorm)
    grad_scan = lax.all_to_all(
        grad_scan_tok.astype(jnp.bfloat16), "head", split_axis=2, concat_axis=1, tiled=True
    )
    grad_scan = grad_scan.astype(jnp.float32).reshape(group_count, tok_span, heads_dev, HEAD_DIM)
    direct = jnp.einsum("gth,gthp,gtn->ghpn", w_cum, grad_scan, query_rows, precision=HIGH)
    grad_query = jnp.einsum("gthp,ghpn,gth->gtn", grad_scan, incoming, w_cum, precision=HIGH)
    grad_wcum = jnp.einsum("gthp,gtn,ghpn->gth", grad_scan, query_rows, incoming, precision=HIGH)
    identity = (jnp.ones_like(carry_gate), jnp.zeros_like(direct))
    later_sum = carried_in((carry_gate, direct), "seq", carry_join, identity)[1]
    grad_gate = jnp.sum(later_sum * incoming, axis=(2, 3))
    unused_scan, pull_scan = jax.vjp(
        lambda ext_in, step_in, taps_in, bias_in, terms_in: local_scan(
            ext_in, step_in, taps_in, bias_in, terms_in, start_ext
        ),
        extended,
        step_float,
        taps_local,
        bias_local,
        head_params,
    )
    grad_ext, grad_step, grad_taps, grad_bias, grad_terms = pull_scan(
        (grad_scan, later_sum, grad_gate, grad_query, grad_wcum)
    )
    rim_grad = passed_along(grad_ext[:, : KW - 1], "seq", -1)
    grad_local = grad_ext[:, KW - 1 :]
    grad_local = grad_local.at[:, tok_span - (KW - 1) :].add(rim_grad)
    grad_x_heads = grad_local[..., :width_dev].astype(jnp.bfloat16)
    grad_shared = grad_local[..., width_dev:]
    grad_x_tok, grad_step_tok = (
        lax.all_to_all(grad_x_heads, "head", split_axis=1, concat_axis=2, tiled=True),
        lax.all_to_all(
            grad_step.astype(jnp.bfloat16), "head", split_axis=1, concat_axis=2, tiled=True
        ),
    )
    grad_shared_tok = lax.psum_scatter(
        grad_shared.astype(jnp.bfloat16), "head", scatter_dimension=1, tiled=True
    )
    grad_proj = jnp.concatenate(
        [grad_gate_in.astype(jnp.bfloat16), grad_x_tok, grad_shared_tok, grad_step_tok], axis=-1
    )
    grad_in = jnp.einsum("gtd,gtk->dk", normed, grad_proj, preferred_element_type=jnp.float32)
    grad_normed = jnp.einsum("gtk,dk->gtd", grad_proj, w_in_b, preferred_element_type=jnp.float32)
    unused_norm, pull_norm = jax.vjp(front_norm, x_float, norm_gain)
    grad_x_float, grad_norm_gain = pull_norm(grad_normed)
    grad_input = (grad_x_float + back_float).astype(jnp.bfloat16)
    conv_full = jnp.zeros((CONV, KW), jnp.float32)
    conv_full = lax.dynamic_update_slice_in_dim(
        conv_full, grad_taps[:width_dev], head_place * width_dev, 0
    )
    conv_full = conv_full.at[INNER:].set(grad_taps[width_dev:])
    bias_full = jnp.zeros((CONV,), jnp.float32)
    bias_full = lax.dynamic_update_slice_in_dim(
        bias_full, grad_bias[:width_dev], head_place * width_dev, 0
    )
    bias_full = bias_full.at[INNER:].set(grad_bias[width_dev:])
    grad_vec_full = jnp.concatenate([grad_norm_gain, bias_full, grad_gate_gain])
    summed = (
        lax.psum_scatter(grad_in, ("seq", "head"), scatter_dimension=0, tiled=True),
        lax.psum_scatter(grad_out, ("seq", "head"), scatter_dimension=0, tiled=True),
        lax.psum_scatter(conv_full, ("seq", "head"), scatter_dimension=0, tiled=True),
        lax.psum_scatter(grad_vec_full, ("seq", "head"), scatter_dimension=0, tiled=True),
    )
    grad_head = lax.psum(grad_terms, "seq")
    in_new = adam(w_in, m_in, v_in, summed[0], rate_input)
    out_new = adam(w_out, m_out, v_out, summed[1], rate_output)
    conv_new = adam(conv_w, m_conv, v_conv, summed[2], rate_conv)
    vec_new = adam(vectors, m_vec, v_vec, summed[3], rate_vector)
    head_new = adam(head_params, m_head, v_head, grad_head, rate_head)
    return (
        result,
        grad_input,
        in_new[0],
        in_new[1],
        in_new[2],
        out_new[0],
        out_new[1],
        out_new[2],
        conv_new[0],
        conv_new[1],
        conv_new[2],
        vec_new[0],
        vec_new[1],
        vec_new[2],
        head_new[0],
        head_new[1],
        head_new[2],
    )


def solution(mesh):
    return jax.shard_map(
        local,
        mesh=mesh,
        in_specs=(
            P(None, ("seq", "head"), None),
            P(),
            P(None, ("seq", "head"), None),
            P(("seq", "head"), None),
            P(("seq", "head"), None),
            P(("seq", "head"), None),
            P(("seq", "head"), None),
            P(("seq", "head"), None),
            P(("seq", "head"), None),
            P(("seq", "head"), None),
            P(("seq", "head"), None),
            P(("seq", "head"), None),
            P(("seq", "head")),
            P(("seq", "head")),
            P(("seq", "head")),
            P(None, "head"),
            P(None, "head"),
            P(None, "head"),
        ),
        out_specs=(
            P(None, ("seq", "head"), None),
            P(None, ("seq", "head"), None),
            P(("seq", "head"), None),
            P(("seq", "head"), None),
            P(("seq", "head"), None),
            P(("seq", "head"), None),
            P(("seq", "head"), None),
            P(("seq", "head"), None),
            P(("seq", "head"), None),
            P(("seq", "head"), None),
            P(("seq", "head"), None),
            P(("seq", "head")),
            P(("seq", "head")),
            P(("seq", "head")),
            P(None, "head"),
            P(None, "head"),
            P(None, "head"),
        ),
        check_vma=False,
    )
```

profile of v0, /device:TPU:0, one launch (start us, length us, event | category | flops | bytes accessed | tf_op | source)
XLA Modules:
  0.0 2170.8 jit_solution(10078144080809639276)
XLA Ops:
  10.8 44.3 %all-reduce.18 = bf16[10496]{0:T(1024)(128)(2,1)S(1)} all-reduce(bf16[10496]{0:T(1024)(128)(2,1)S(1)} %dynamic-update-slice.8), channel_id=1, replica_groups=mesh['seq'=8,'head'=4] {'seq','head'}, use_global_device_ids=true, to_apply=%add.18 | all-reduce | flops 10496 | bytes 41984
  58.6 41.9 %all-gather.4 = bf16[32,136,4]{1,2,0:T(4,128)(2,1)S(1)} all-gather(bf16[1,136,4]{1,2,0:T(4,128)(2,1)S(1)} %convert_bitcast_fusion.2), channel_id=1, replica_groups=mesh['seq'=8,'head'=4] {'seq','head'}, dimensions={0}, use_global_device_ids=true | all-gather | bytes 35904 | tf_op jit(solution)/shard_map/all_gather | solution.py:222
  103.5 114.9 %all-gather.10.cloned.1.call-done = bf16[2048,8512]{1,0:T(8,128)(2,1)} async-done(((bf16[64,8512]{1,0:T(8,128)(2,1)}), bf16[2048,8512]{1,0:T(8,128)(2,1)}) %all-gather.10.cloned.1.call-update) | async-done | bytes 34865168 | tf_op jit(solution)/shard_map/all_gather | solution.py:220
  218.5 18.1 fusion.167
  306.9 19.1 all-gather
  327.6 12.2 fusion.17
  339.8 86.5 %all-gather.14.cloned.1.call-done = f32[16,16,64,128]{3,2,1,0:T(8,128)} async-done(((f32[2,16,64,128]{3,2,1,0:T(8,128)}), f32[16,16,64,128]{3,2,1,0:T(8,128)}) %all-gather.14.cloned.1.call-update) | async-done | bytes 8388624 | tf_op jit(solution)/shard_map/all_gather | solution.py:38
  444.8 14.4 all-to-all-done.2
  465.7 13.2 convolution_bitcast_fusion.1
  478.9 370.3 %reduce-scatter.9.cloned.1.call-done = f32[128,2048]{1,0:T(8,128)} async-done(((f32[4096,2048]{1,0:T(8,128)}), f32[128,2048]{1,0:T(8,128)}) %reduce-scatter.9.cloned.1.call-update) | async-done | bytes 1048592 | tf_op jit(solution)/shard_map/reduce_scatter | solution.py:386
  854.8 122.5 %all-gather.12.cloned.1.call-done = bf16[4096,2048]{1,0:T(8,128)(2,1)} async-done(((bf16[128,2048]{1,0:T(8,128)(2,1)}), bf16[4096,2048]{1,0:T(8,128)(2,1)}) %all-gather.12.cloned.1.call-update) | async-done | bytes 16777232 | tf_op jit(solution)/shard_map/all_gather | solution.py:221
  977.2 14.3 multiply_reduce_fusion.5
  1007.6 18.8 all_to_all.102
  1049.6 19.0 all-gather.3
  1088.8 31.2 %all-gather.16.cloned.1.call-done = bf16[16,16,64,128]{3,2,1,0:T(8,128)(2,1)} async-done(((bf16[2,16,64,128]{3,2,1,0:T(8,128)(2,1)}), bf16[16,16,64,128]{3,2,1,0:T(8,128)(2,1)}) %all-gather.16.cloned.1.call-update) | async-done | bytes 4194320 | tf_op jit(solution)/shard_map/all_gather | solution.py:52
  1119.9 25.5 %while.22 = (s32[]{:T(128)}, f32[2,16,64,128]{3,2,1,0:T(8,128)}, s32[]{:T(128)}, bf16[8,2,16]{2,1,0:T(2,128)(2,1)}, bf16[8,2,16,64,128]{4,3,2,1,0:T(8,128)(2,1)}...) while((s32[]{:T(128)}, f32[2,16,64,128]{3,2,1,0:T(8,128)}, s32[]{:T(128)}, ...), condition=%wide.region_14.15_spmd.clone, body=%wide.region_13.14_spmd.clone.sunk | while | flops 1310760 | bytes 2621935 | solution.py:70
  1177.6 14.4 fusion.23
  1268.4 11.4 all-to-all-done.4
  1289.8 25.6 %convolution_bitcast_fusion = f32[2048,8512]{1,0:T(8,128)} fusion(bf16[2,64,2048]{2,1,0:T(8,128)(2,1)S(1)} %copy-done.16, f32[2048]{0:T(1024)S(1)} %slice.382, f32[2,64]{1,0:T(2,128)S(1)} %fusion.140, bf16[2,64,64]{2,1,0:T(8,128)(2,1)S(1)} %copy.267, bf16[2,64,256]{2,1,0:T(8,128)(2,1)} %reduce-scatter.5.cloned.1.call-done, ...), kind=kOutput, calls=%fused_computation.5 | convolution fusion | flops 4472504320 | bytes 72442368 | tf_op jit(solution)/shard_map/gtd,gtk->dk/dot_general | solution.py:368
  1326.7 21.6 psum.7
  1349.0 65.8 %all-reduce.23.cloned.1.call-done = f32[4352,4]{0,1:T(4,128)} async-done(((f32[4352,4]{0,1:T(4,128)}), f32[4352,4]{0,1:T(4,128)}) %all-reduce.23.cloned.1.call-update) | async-done | bytes 69648
  1416.2 18.8 fusion.97
  1435.1 48.8 %all-reduce.20 = f32[10496]{0:T(1024)S(1)} all-reduce(f32[10496]{0:T(1024)S(1)} %pad_maximum_fusion.3), channel_id=10, replica_groups=mesh['seq'=8,'head'=4] {'seq','head'}, use_global_device_ids=true, to_apply=%region_43.44.clone | all-reduce | flops 10496 | bytes 83968
  1487.2 668.6 %reduce-scatter.7.cloned.1.call-done = f32[64,8512]{1,0:T(8,128)} async-done(((f32[2048,8512]{1,0:T(8,128)}), f32[64,8512]{1,0:T(8,128)}) %reduce-scatter.7.cloned.1.call-update) | async-done | bytes 2179088 | tf_op jit(solution)/shard_map/reduce_scatter | solution.py:385
  (468 shorter events, 339.3 us)
Async XLA Ops:
  7.2 211.2 %all-gather.10.cloned.1.call-start = ((), (), s32[]{:S(2)}) async-start(), calls=%async_computation.9 | async-start | bytes 36225024 | tf_op jit(solution)/shard_map/all_gather | solution.py:220
  56.2 180.3 %copy-start.71 = (s32[1,2,2,128]{3,1,2,0:T(2,128)}, s32[1,2,2,128]{3,1,2,0:T(2,128)S(1)}, u32[]{:S(2)}) copy-start(s32[1,2,2,128]{3,1,2,0:T(2,128)S(1)} %copy.323) | copy-start | bytes 6148
  57.4 204.0 %copy-start.31 = (f32[2,256]{0,1:T(8,128)}, f32[2,256]{0,1:T(8,128)S(1)}, u32[]{:S(2)}) copy-start(f32[2,256]{0,1:T(8,128)S(1)} %copy.231) | copy-start | bytes 6148
  102.1 186.1 %copy-start.51 = (f32[1280]{0:T(1024)}, f32[1280]{0:T(1024)S(1)}, u32[]{:S(2)}) copy-start(f32[1280]{0:T(1024)S(1)} %get-tuple-element.407) | copy-start | bytes 15364
  102.1 186.1 %copy-start.53 = (f32[1280]{0:T(1024)}, f32[1280]{0:T(1024)S(1)}, u32[]{:S(2)}) copy-start(f32[1280]{0:T(1024)S(1)} %get-tuple-element.408) | copy-start | bytes 15364
  102.3 134.2 %copy-start.83 = (f32[2,64]{1,0:T(2,128)}, f32[2,64]{1,0:T(2,128)S(1)}, u32[]{:S(2)}) copy-start(f32[2,64]{1,0:T(2,128)S(1)} %fusion.101) | copy-start | bytes 1540
  102.9 156.7 %copy-start.89 = (f32[16]{0:T(128)}, f32[16]{0:T(128)S(1)}, u32[]{:S(2)}) copy-start(f32[16]{0:T(128)S(1)} %get-tuple-element.484) | copy-start | bytes 196
  102.9 156.7 %copy-start.90 = (f32[16]{0:T(128)}, f32[16]{0:T(128)S(1)}, u32[]{:S(2)}) copy-start(f32[16]{0:T(128)S(1)} %get-tuple-element.485) | copy-start | bytes 196
  103.5 184.7 %copy-start.64 = (f32[2,256]{1,0:T(2,128)}, f32[2,256]{1,0:T(2,128)S(1)}, u32[]{:S(2)}) copy-start(f32[2,256]{1,0:T(2,128)S(1)} %get-tuple-element.478) | copy-start | bytes 6148
  237.4 18.3 all-to-all-start.1
  255.6 18.1 all-to-all-start
  259.3 167.0 %all-gather.14.cloned.1.call-start = ((), (), s32[]{:S(2)}) async-start(), calls=%async_computation.14 | async-start | bytes 9437184 | tf_op jit(solution)/shard_map/all_gather | solution.py:38
  281.1 5.5 collective-permute-start
  440.5 18.8 all-to-all-start.2
  444.7 404.5 %reduce-scatter.9.cloned.1.call-start = ((), (), s32[]{:S(2)}) async-start(), calls=%async_computation.13 | async-start | bytes 34603008 | tf_op jit(solution)/shard_map/reduce_scatter | solution.py:386
  478.9 498.3 %all-gather.12.cloned.1.call-start = ((), (), s32[]{:S(2)}) async-start(), calls=%async_computation.10 | async-start | bytes 17301504 | tf_op jit(solution)/shard_map/all_gather | solution.py:221
  854.5 265.4 %all-gather.16.cloned.1.call-start = ((), (), s32[]{:S(2)}) async-start(), calls=%async_computation.15 | async-start | bytes 4718592 | tf_op jit(solution)/shard_map/all_gather | solution.py:52
  1246.2 9.8 collective-permute-start.1
  1249.9 11.9 all-to-all-start.5
  1261.8 18.0 all-to-all-start.4
  1265.3 24.5 %reduce-scatter.5.cloned.1.call-start = ((), (), s32[]{:S(2)}) async-start(), calls=%async_computation.11 | async-start | bytes 327680 | tf_op jit(solution)/shard_map/reduce_scatter | solution.py:362
  1267.2 147.6 %all-reduce.23.cloned.1.call-start = ((), (), s32[]{:S(2)}) async-start(), calls=%async_computation.16 | async-start | bytes 139264
  1268.0 887.8 %reduce-scatter.7.cloned.1.call-start = ((), (), s32[]{:S(2)}) async-start(), calls=%async_computation.12 | async-start | bytes 72450048 | tf_op jit(solution)/shard_map/reduce_scatter | solution.py:385
  1435.0 720.7 %copy-start.19 = (f32[64,8512]{1,0:T(8,128)S(1)}, f32[64,8512]{1,0:T(8,128)}, u32[]{:S(2)}) copy-start(f32[64,8512]{1,0:T(8,128)} %param.31) | copy-start | bytes 6537220
  (94 other events, 1646.7 us)
Sparse Core Ops, SparseCore 0:
  11.5 206.8 all-gather.9
  302.9 123.3 all-gather.13
  479.0 370.1 reduce-scatter.8
  854.7 122.5 all-gather.11
  1048.3 71.6 all-gather.15
  1268.9 20.8 reduce-scatter.4
  1296.9 117.8 all-reduce.22
  1417.3 738.4 reduce-scatter.6
where the time goes:
time: 2190 us; the launch traced here: 2170 us
  waiting for transfers between devices  1510 us (69%)
  blocking collectives  220 us (10%)
  matrix products  180 us (8%)
  other arithmetic  119 us (5%)
  local copies, waits for them, and re-layouts  107 us (5%)
  starting transfers between devices  23.9 us (1%)
    reduce_scatter x1, waiting for transfers between devices, local(): lax.psum_scatter(grad_in, ('seq', 'head'), scatter_dimension=0, tiled=True)  669 us
    reduce_scatter x1, waiting for transfers between devices, local(): lax.psum_scatter(grad_out, ('seq', 'head'), scatter_dimension=0, tiled=True)  370 us
    all_gather x1, waiting for transfers between devices, local(): lax.all_gather(w_out.astype(jnp.bfloat16), ('seq', 'head'), axis=0, tiled...  122 us
    all_gather x1, waiting for transfers between devices, local(): lax.all_gather(w_in.astype(jnp.bfloat16), ('seq', 'head'), axis=0, tiled=...  115 us
    unnamed x2, blocking collectives  93.1 us
    all_gather x1, waiting for transfers between devices, prefix(): gathered = jax.tree.map(lambda a: lax.all_gather(a, axis), part)  86.5 us
    unnamed x9, waiting for transfers between devices  65.9 us
  transfers between devices with their start and end apart: 15, of which 11 were waited for; matrix products, arithmetic and copies ran while one was open for 6% of the time, Pallas kernels for 0%

commit v1 on v0

v1 whole, which is shorter than its diff:
```python
import functools

import jax
import jax.numpy as jnp
from jax import lax
from jax.experimental import pallas as pl
from jax.experimental.pallas import tpu as pltpu
from jax.sharding import Mesh
from jax.sharding import PartitionSpec as P

D = 2048
HEADS = 64
HEAD_DIM = 64
STATE = 128
KW = 4
STEP = 4
INNER = 4096
CONV = 4352
MIX = 2 * STATE
SMALL = 384
CHUNK = 128
EDGE = 16

EPS = 1e-05
BETA_ONE = 0.5
BETA_TWO = 0.7
ADAM_EPS = 1e-08
DECAY = 0.1
rate_input = 0.02
rate_output = 0.015
rate_conv = 0.3
rate_vector = 0.5
rate_head = 0.5
HIGH = lax.Precision.HIGHEST
f32 = jnp.float32
bf16 = jnp.bfloat16
Q = ("y", "head")
ALL = ("z", "y", "head")
VMEM_LIMIT = 48 * 1024 * 1024


def dot(a, b, on_a=1, on_b=0):
    return lax.dot_general(
        a.astype(bf16), b.astype(bf16), (((on_a,), (on_b,)), ((), ())), preferred_element_type=f32
    )


def dot_exact(a, b, on_a=1, on_b=0):
    return lax.dot_general(
        a, b, (((on_a,), (on_b,)), ((), ())), preferred_element_type=f32, precision=HIGH
    )


def sigmoid(v):
    return 1.0 / (1.0 + jnp.exp(-v))


def softplus(v):
    return jnp.maximum(v, 0.0) + jnp.log1p(jnp.exp(-jnp.abs(v)))


def places(first, count, axis):
    shape = (count, 1) if axis == 0 else (1, count)
    return first + lax.broadcasted_iota(jnp.int32, shape, axis)


def segment(offsets, group, spots, sequences):
    total = jnp.zeros_like(spots)
    for k in range(sequences):
        total = total + (spots >= offsets[group, k]).astype(jnp.int32)
    return total


def lagged(current, before, own_seg, lag_segs):
    whole = jnp.concatenate([before, current], axis=0)
    rows = current.shape[0]
    edge = before.shape[0]
    out = []
    for lag in range(1, KW):
        keep = (own_seg == lag_segs[lag - 1]).astype(f32)
        out.append(whole[edge - lag : edge - lag + rows] * keep)
    return out


def conv(current, lags, taps):
    total = taps[4:5] + taps[3:4] * current
    for lag in range(1, KW):
        total = total + taps[3 - lag : 4 - lag] * lags[lag - 1]
    return total


class Place:
    def __init__(self, offsets, group, chunk, sequences):
        first = chunk * CHUNK
        at = places(first, CHUNK, 0)
        seg = functools.partial(segment, offsets, group, sequences=sequences)
        self.col = seg(at)
        self.row = seg(places(first, CHUNK, 1))
        self.lags = [seg(at - lag) for lag in range(1, KW)]
        self.ahead = [seg(at + lag) for lag in range(1, KW)]
        self.before = seg(places(first - 1, 1, 0))
        self.last = seg(places(first + CHUNK - 1, 1, 0))
        self.fresh = (self.col == self.before).astype(f32)
        self.open_end = (self.col == self.last).astype(f32)
        self.unbroken = (self.last == self.before).astype(f32)


def rows_of(ref):
    block = ref[...]
    return block.reshape(CHUNK, block.shape[-1])


def steps_of(small, pick, hp):
    raw = dot(small[:, MIX:], pick)
    shifted = raw + hp[0:1]
    step = softplus(shifted)
    log_a = -jnp.exp(hp[1:2]) * step
    lower = (
        lax.broadcasted_iota(jnp.int32, (CHUNK, CHUNK), 0)
        >= lax.broadcasted_iota(jnp.int32, (CHUNK, CHUNK), 1)
    ).astype(f32)
    running = dot_exact(lower, log_a)
    return shifted, step, log_a, running, lower


def state_kernel(sequences, offs, x, xp, xh, s, sp, sh, tx, ts, hp, pick, spread, out, carry, fall):
    group, chunk = pl.program_id(0), pl.program_id(1)
    place = Place(offs, group, chunk, sequences)

    @pl.when(chunk == 0)
    def _():
        carry[...] = jnp.zeros_like(carry)
        fall[...] = jnp.ones_like(fall)

    small = rows_of(s)
    xs = rows_of(x).astype(f32)
    prev = jnp.where(chunk == 0, xh[0], xp[0, 0]).astype(f32)
    act = conv(xs, lagged(xs, prev, place.col, place.lags), tx[...])
    values = act * sigmoid(act)
    bs = small[:, :STATE].astype(f32)
    prev_b = jnp.where(chunk == 0, sh[0], sp[0, 0])[:, :STATE].astype(f32)
    act_b = conv(bs, lagged(bs, prev_b, place.col, place.lags), ts[:, :STATE])
    keys = act_b * sigmoid(act_b)
    _, step, _, running, _ = steps_of(small, pick[...], hp[...])
    end = running[CHUNK - 1 : CHUNK]
    weight = jnp.exp(end - running) * place.open_end * step
    carried = dot_exact(jnp.broadcast_to(jnp.exp(end) * place.unbroken, (8, 128)), spread[...])[0:1]
    memory = carried * carry[...] + dot(keys, values * dot_exact(weight, spread[...]), 0, 0)
    total = fall[0:1] * carried
    carry[...] = memory
    fall[...] = jnp.broadcast_to(total, fall.shape)

    @pl.when(chunk == pl.num_programs(1) - 1)
    def _():
        high = total.astype(bf16)
        middle = (total - high.astype(f32)).astype(bf16)
        low = (total - high.astype(f32) - middle.astype(f32)).astype(bf16)
        out[0, :STATE] = memory.astype(bf16)
        out[0, STATE:] = jnp.concatenate(
            [high, middle, low, jnp.zeros((EDGE - 3, high.shape[1]), bf16)], axis=0
        )


def scan_kernel(sequences, offs, x, xp, xh, s, sp, sh, tx, ts, hp, pick, spread, first, out, kept, carry):
    group, chunk = pl.program_id(0), pl.program_id(1)
    place = Place(offs, group, chunk, sequences)

    @pl.when(chunk == 0)
    def _():
        carry[...] = first[0]

    memory = carry[...]
    kept[0, 0] = memory
    small = rows_of(s)
    xs = rows_of(x).astype(f32)
    prev = jnp.where(chunk == 0, xh[0], xp[0, 0]).astype(f32)
    act = conv(xs, lagged(xs, prev, place.col, place.lags), tx[...])
    values = act * sigmoid(act)
    mix = small[:, :MIX].astype(f32)
    prev_m = jnp.where(chunk == 0, sh[0], sp[0, 0])[:, :MIX].astype(f32)
    act_m = conv(mix, lagged(mix, prev_m, place.col, place.lags), ts[...])
    act_m = act_m * sigmoid(act_m)
    keys, queries = act_m[:, :STATE], act_m[:, STATE:]
    _, step, _, running, lower = steps_of(small, pick[...], hp[...])
    end = running[CHUNK - 1 : CHUNK]
    inflow = jnp.exp(running) * place.fresh
    weight = jnp.exp(end - running) * place.open_end
    carried = jnp.exp(end) * place.unbroken
    wide = dot_exact(
        jnp.concatenate([step, inflow, weight, jnp.broadcast_to(carried, (8, 128)), hp[...]], axis=0),
        spread[...],
    )
    step_w, inflow_w, weight_w = (wide[i * CHUNK : (i + 1) * CHUNK] for i in range(3))
    carried_w = wide[3 * CHUNK : 3 * CHUNK + 1]
    skip_w = wide[3 * CHUNK + 10 : 3 * CHUNK + 11]
    weighted = values * step_w
    within = (place.col == place.row) & (lower > 0.5)
    scores = dot(queries, keys, 1, 1)
    running_t = running.T
    left = lax.broadcasted_iota(jnp.int32, (1, 128), 1) < HEAD_DIM
    from_memory = dot(queries, memory) * inflow_w + skip_w * values
    for pair in range(values.shape[1] // 128):
        lanes = slice(128 * pair, 128 * pair + 128)
        mixed = []
        for h in (2 * pair, 2 * pair + 1):
            gaps = running[:, h : h + 1] - running_t[h : h + 1, :]
            mixed.append(scores * jnp.exp(jnp.where(within, gaps, -1e30)))
        part = weighted[:, lanes]
        both = jnp.concatenate([jnp.where(left, part, 0.0), jnp.where(left, 0.0, part)], axis=0)
        result = dot(jnp.concatenate(mixed, axis=1), both) + from_memory[:, lanes]
        out[:, 0, :, lanes] = result.astype(bf16).reshape(out.shape[0], out.shape[2], 128)
    carry[...] = carried_w * memory + dot(keys, weighted * weight_w, 0, 0)


def direct_kernel(sequences, offs, s, sp, sh, ts, hp, pick, spread, dy, out, carry, fall):
    group, chunk = pl.program_id(0), pl.program_id(1)
    place = Place(offs, group, chunk, sequences)

    @pl.when(chunk == 0)
    def _():
        carry[...] = jnp.zeros_like(carry)
        fall[...] = jnp.ones_like(fall)

    small = rows_of(s)
    cs = small[:, STATE:MIX].astype(f32)
    prev_c = jnp.where(chunk == 0, sh[0], sp[0, 0])[:, STATE:MIX].astype(f32)
    act_c = conv(cs, lagged(cs, prev_c, place.col, place.lags), ts[:, STATE:])
    queries = act_c * sigmoid(act_c)
    _, _, _, running, _ = steps_of(small, pick[...], hp[...])
    end = running[CHUNK - 1 : CHUNK]
    wide = dot_exact(
        jnp.concatenate(
            [
                jnp.exp(running) * place.fresh,
                jnp.broadcast_to(jnp.exp(end) * place.unbroken, (8, 128)),
            ],
            axis=0,
        ),
        spread[...],
    )
    grad = rows_of(dy).astype(f32) * wide[:CHUNK]
    total = carry[...] + fall[0:1] * dot(queries, grad, 0, 0)
    carry[...] = total
    fall[...] = fall[...] * wide[CHUNK : CHUNK + 1]

    @pl.when(chunk == pl.num_programs(1) - 1)
    def _():
        out[0] = total.astype(bf16)


def conv_back(du, ahead, taps, own_seg, ahead_segs):
    rows = du.shape[0]
    whole = jnp.concatenate([du, ahead], axis=0)
    total = taps[3:4] * du
    for lag in range(1, KW):
        keep = (own_seg == ahead_segs[lag - 1]).astype(f32)
        total = total + taps[3 - lag : 4 - lag] * (whole[lag : lag + rows] * keep)
    return total


def conv_rim(du, taps, seg):
    at = places(-EDGE, EDGE, 0)
    whole = jnp.concatenate([jnp.zeros((EDGE, du.shape[1]), f32), du[:EDGE]], axis=0)
    total = jnp.zeros((EDGE, du.shape[1]), f32)
    for lag in range(1, KW):
        keep = (seg(at) == seg(at + lag)).astype(f32)
        total = total + taps[3 - lag : 4 - lag] * (whole[lag : lag + EDGE] * keep)
    return total


def column_sums(du, current, lags):
    rows = [jnp.sum(du * lags[KW - 2 - k], axis=0, keepdims=True) for k in range(KW - 1)]
    rows.append(jnp.sum(du * current, axis=0, keepdims=True))
    rows.append(jnp.sum(du, axis=0, keepdims=True))
    return rows


def back_kernel(
    sequences, offs, x, xp, xh, s, sp, sh, tx, ts, hp, pick, spread, dy, kept, later,
    dx, ds, tail_x, tail_s, rim_x, rim_s, gx, gs, gh, carry, next_x, next_s,
):
    group = pl.program_id(0)
    chunks = pl.num_programs(1)
    chunk = chunks - 1 - pl.program_id(1)
    place = Place(offs, group, chunk, sequences)
    seg = functools.partial(segment, offs, group, sequences=sequences)
    width = tx.shape[1]
    head_count = width // HEAD_DIM

    @pl.when(pl.program_id(1) == 0)
    def _():
        carry[...] = later[0]
        next_x[...] = jnp.zeros_like(next_x)
        next_s[...] = jnp.zeros_like(next_s)

    @pl.when((pl.program_id(1) == 0) & (group == 0))
    def _():
        gx[...] = jnp.zeros_like(gx)
        gs[...] = jnp.zeros_like(gs)
        gh[...] = jnp.zeros_like(gh)

    small = rows_of(s)
    xs = rows_of(x).astype(f32)
    prev = jnp.where(chunk == 0, xh[0], xp[0, 0]).astype(f32)
    lags_x = lagged(xs, prev, place.col, place.lags)
    act = conv(xs, lags_x, tx[...])
    gate = sigmoid(act)
    values = act * gate
    slope_x = gate * (1.0 + act * (1.0 - gate))
    mix = small[:, :MIX].astype(f32)
    prev_m = jnp.where(chunk == 0, sh[0], sp[0, 0])[:, :MIX].astype(f32)
    lags_m = lagged(mix, prev_m, place.col, place.lags)
    act_m = conv(mix, lags_m, ts[...])
    gate_m = sigmoid(act_m)
    keys, queries = (act_m * gate_m)[:, :STATE], (act_m * gate_m)[:, STATE:]
    slope_m = gate_m * (1.0 + act_m * (1.0 - gate_m))
    shifted, step, log_a, running, lower = steps_of(small, pick[...], hp[...])
    end = running[CHUNK - 1 : CHUNK]
    carried = jnp.exp(end) * place.unbroken
    wide = dot_exact(
        jnp.concatenate(
            [
                step,
                jnp.exp(running) * place.fresh,
                jnp.exp(end - running) * place.open_end,
                jnp.broadcast_to(carried, (8, 128)),
                hp[...],
            ],
            axis=0,
        ),
        spread[...],
    )
    step_w, inflow_w, weight_w = (wide[i * CHUNK : (i + 1) * CHUNK] for i in range(3))
    carried_w = wide[3 * CHUNK : 3 * CHUNK + 1]
    skip_w = wide[3 * CHUNK + 10 : 3 * CHUNK + 11]
    grad = rows_of(dy).astype(f32)
    weighted = values * step_w
    memory = kept[0, 0]
    back = carry[...]

    scores = dot(queries, keys, 1, 1)
    running_t = running.T
    within = (place.col == place.row) & (lower > 0.5)
    left = lax.broadcasted_iota(jnp.int32, (1, 128), 1) < HEAD_DIM
    lane = lax.broadcasted_iota(jnp.int32, (1, 128), 1)

    grad_in = grad * inflow_w
    to_end = weighted * weight_w
    back_values = dot(keys, back) * weight_w
    from_state = weighted * back_values
    grad_run = grad_in * dot(queries, memory) - from_state
    grad_scores = jnp.zeros((CHUNK, CHUNK), f32)
    run_cols = jnp.zeros((CHUNK, 128), f32)
    run_rows = []
    back_weighted = []
    for pair in range(width // 128):
        lanes = slice(128 * pair, 128 * pair + 128)
        decays = []
        for h in (2 * pair, 2 * pair + 1):
            gaps = running[:, h : h + 1] - running_t[h : h + 1, :]
            decays.append(jnp.exp(jnp.where(within, gaps, -1e30)))
        decay = jnp.concatenate(decays, axis=0)
        mixed = jnp.concatenate([scores, scores], axis=0) * decay
        part = grad[:, lanes]
        both = jnp.concatenate([jnp.where(left, part, 0.0), jnp.where(left, 0.0, part)], axis=0)
        grad_mixed = dot(both, weighted[:, lanes], 1, 1)
        through = grad_mixed * decay
        grad_scores = grad_scores + through[:CHUNK] + through[CHUNK:]
        pull = grad_mixed * mixed
        sums = jnp.sum(pull, axis=1, keepdims=True)
        run_cols = run_cols + jnp.where(lane == 2 * pair, sums[:CHUNK], 0.0)
        run_cols = run_cols + jnp.where(lane == 2 * pair + 1, sums[CHUNK:], 0.0)
        run_rows.append(jnp.sum(pull[:CHUNK], axis=0, keepdims=True))
        run_rows.append(jnp.sum(pull[CHUNK:], axis=0, keepdims=True))
        back_weighted.append(dot(mixed, both, 0, 0) + back_values[:, lanes])
    back_weighted = jnp.concatenate(back_weighted, axis=1)
    run_rows.append(jnp.zeros((CHUNK - head_count, CHUNK), f32))
    run_cols = run_cols - jnp.concatenate(run_rows, axis=0).T

    grad_queries = dot(grad_scores, keys) + dot(grad_in, memory, 1, 1)
    grad_keys = dot(grad_scores, queries, 0, 0) + dot(to_end, back, 1, 1)
    end_sum = jnp.sum(from_state, axis=0, keepdims=True) + carried_w * jnp.sum(
        back * memory, axis=0, keepdims=True
    )
    carry[...] = carried_w * back + dot(queries, grad_in, 0, 0)

    narrow = dot_exact(
        jnp.concatenate(
            [grad_run, back_weighted * values, jnp.broadcast_to(end_sum, (8, width))], axis=0
        ),
        spread[...],
        1,
        1,
    )
    grad_log = dot_exact(lower, run_cols + narrow[:CHUNK], 0, 0) + narrow[2 * CHUNK : 2 * CHUNK + 1]
    rate = -jnp.exp(hp[1:2])
    grad_step = (narrow[CHUNK : 2 * CHUNK] + grad_log * rate) * sigmoid(shifted)
    gh[0:1] += jnp.sum(grad_step, axis=0, keepdims=True)
    gh[1:2] += jnp.sum(grad_log * log_a, axis=0, keepdims=True)

    du_x = (back_weighted * step_w + skip_w * grad) * slope_x
    du_m = jnp.concatenate([grad_keys, grad_queries], axis=1) * slope_m
    rows = column_sums(du_x, xs, lags_x)
    rows.append(jnp.sum(grad * values, axis=0, keepdims=True))
    rows.append(jnp.zeros((2, width), f32))
    gx[...] += jnp.concatenate(rows, axis=0)
    rows = column_sums(du_m, mix, lags_m)
    rows.append(jnp.zeros((3, MIX), f32))
    gs[...] += jnp.concatenate(rows, axis=0)

    grad_x = conv_back(du_x, next_x[...], tx[...], place.col, place.ahead)
    grad_m = conv_back(du_m, next_s[...], ts[...], place.col, place.ahead)
    next_x[...] = du_x[:8]
    next_s[...] = du_m[:8]
    shape = (dx.shape[0], dx.shape[2])
    dx[:, 0] = grad_x.astype(bf16).reshape(shape + (width,))
    ds[:, 0, :, :MIX] = grad_m.astype(bf16).reshape(shape + (MIX,))
    placed = dot(grad_step, pick[...], 1, 1)
    ds[:, 0, :, MIX:] = placed.astype(bf16).reshape(shape + (SMALL - MIX,))

    @pl.when(chunk == chunks - 1)
    def _():
        tail_x[0] = grad_x[CHUNK - EDGE :]
        tail_s[0] = grad_m[CHUNK - EDGE :]

    @pl.when(chunk == 0)
    def _():
        rim_x[0] = conv_rim(du_x, tx[...], seg)
        rim_s[0] = conv_rim(du_m, ts[...], seg)


def adam(weight, first, second, grad, rate):
    first_new = BETA_ONE * first + (1.0 - BETA_ONE) * grad
    second_new = BETA_TWO * second + (1.0 - BETA_TWO) * grad * grad
    update = (
        first_new
        / (1.0 - BETA_ONE**STEP)
        / (jnp.sqrt(second_new / (1.0 - BETA_TWO**STEP)) + ADAM_EPS)
    )
    return (weight - rate * (update + DECAY * weight), first_new, second_new)


def shifted_along(value, axis, by):
    peers = lax.axis_size(axis)
    pairs = [(i, i + by) for i in range(peers) if 0 <= i + by < peers]
    return lax.ppermute(value, axis, pairs)


def three_parts(value):
    high = lax.reduce_precision(value, 8, 7)
    middle = lax.reduce_precision(value - high, 8, 7)
    low = value - high - middle
    return jnp.stack([high, middle, low]).astype(bf16)


def product(a, b, on_a, on_b):
    return lax.dot_general(a, b, (((on_a,), (on_b,)), ((), ())), preferred_element_type=f32)


def local(
    x_in, lengths, cotangent, w_in, m_in, v_in, w_out, m_out, v_out, conv_w, m_conv, v_conv,
    vectors, m_vec, v_vec, head_params, m_head, v_head,
):
    zn = lax.axis_size("z")
    head_size = lax.axis_size("head")
    qn = lax.axis_size("y") * head_size
    devices = zn * qn
    q = lax.axis_index(Q)
    z = lax.axis_index("z")
    groups, own, _ = x_in.shape
    span = own * qn
    sequences = lengths.shape[1]
    chunks = span // CHUNK
    part = CHUNK // own
    tokens = groups * span
    width = INNER // qn
    heads_own = HEADS // qn
    unit = INNER // devices
    strided = unit % HEAD_DIM == 0
    rows_in = D // devices
    conv_rows, vec_rows, head_cols = conv_w.shape[0], vectors.shape[0], head_params.shape[1]

    def split(array, size):
        lead = array.shape[:-1]
        if strided:
            array = array.reshape(lead + (zn, qn, size // devices))
        else:
            array = array.reshape(lead + (1, qn, size // qn))
        return jnp.moveaxis(array, -2, 0).reshape((qn,) + lead + (size // qn,))

    def join(array, size):
        lead = array.shape[1:-1]
        count = zn if strided else 1
        array = array.reshape((qn,) + lead + (count, size // (qn * count)))
        return jnp.moveaxis(array, 0, -2).reshape(lead + (size,))

    def own_of(array, size):
        return lax.dynamic_index_in_dim(split(array, size), q, 0, False)

    own_heads = own_of(jnp.arange(HEADS, dtype=jnp.int32), HEADS)

    payload = jnp.concatenate(
        [
            conv_w.astype(bf16).T.reshape(-1),
            vectors.astype(bf16),
            three_parts(head_params).reshape(-1),
        ]
    )
    payload = jnp.pad(payload, (0, rows_in * HEADS - payload.shape[0])).reshape(rows_in, HEADS)
    small_own = jnp.concatenate([w_in[:, 2 * INNER :].astype(bf16), payload], axis=1)
    small_all = lax.all_gather(small_own, ALL, axis=0, tiled=False)
    w_small = small_all.reshape(D, SMALL)
    payload = small_all[:, :, SMALL - HEADS :].reshape(devices, rows_in * HEADS)
    cut = [conv_rows * KW, vec_rows, 9 * head_cols]
    taps = jnp.moveaxis(payload[:, : cut[0]].reshape(devices, KW, conv_rows), 0, 1)
    taps = taps.reshape(KW, CONV).astype(f32)
    vec = payload[:, cut[0] : cut[0] + cut[1]].reshape(-1).astype(f32)
    params = payload[:head_size, cut[0] + cut[1] : sum(cut)].astype(f32)
    params = jnp.sum(params.reshape(head_size, 3, 3, head_cols), axis=1)
    params = jnp.moveaxis(params, 0, 1).reshape(3, HEADS)
    norm_gain = vec[:D]
    conv_bias = vec[D : D + CONV]
    gate_gain = own_of(vec[D + CONV :], INNER)
    table = jnp.concatenate([taps, conv_bias[None], jnp.zeros((3, CONV), f32)], axis=0)
    taps_x = own_of(table[:, :INNER], INNER)
    taps_s = table[:, INNER:]
    lanes = jnp.arange(128, dtype=jnp.int32)
    head_of_lane = jnp.pad(own_heads, (0, 128 - heads_own), constant_values=-1)
    pick = (lanes[:, None] == head_of_lane[None, :]).astype(bf16)
    hp = jnp.sum(
        jnp.where(jnp.arange(HEADS)[:, None] == head_of_lane[None, :], params[:, :, None], 0.0), 1
    )
    hp = jnp.pad(hp, ((0, 5), (0, 0)))
    spread = (lanes[:, None] == jnp.arange(width)[None, :] // HEAD_DIM).astype(f32)
    offsets = (jnp.cumsum(lengths, axis=1) - lengths - z * span).astype(jnp.int32)

    x_all = lax.all_gather(x_in, Q, axis=0, tiled=False).reshape(tokens, D)
    cot_all = lax.all_gather(cotangent, Q, axis=0, tiled=False).reshape(tokens, D)

    def columns(first):
        mine = split(w_in[:, first : first + INNER].astype(bf16), INNER)
        mine = lax.all_to_all(mine, Q, split_axis=0, concat_axis=0, tiled=True)
        return lax.all_gather(mine, "z", axis=0, tiled=False).reshape(D, width)

    w_x = columns(INNER)
    w_z = columns(0)
    if strided:
        w_o = lax.all_gather(w_out.astype(bf16), "z", axis=0, tiled=True)
    else:
        w_o = lax.all_gather(w_out.astype(bf16), ALL, axis=0, tiled=True)
        w_o = lax.dynamic_slice_in_dim(w_o, q * width, width, 0)

    x_float = x_all.astype(f32)
    x_scaled = x_float * lax.rsqrt(jnp.mean(x_float * x_float, axis=-1, keepdims=True) + EPS)
    normed = (x_scaled * norm_gain).astype(bf16)
    token_shape = (qn, groups, own)
    x_raw = product(normed, w_x, 1, 0).astype(bf16).reshape(token_shape + (width,))
    s_raw = product(normed, w_small, 1, 0).astype(bf16).reshape(token_shape + (SMALL,))
    x_halo = shifted_along(x_raw[qn - 1, :, own - EDGE :], "z", 1)
    s_halo = shifted_along(s_raw[qn - 1, :, own - EDGE :], "z", 1)

    def at(reverse):
        return (lambda i: chunks - 1 - i) if reverse else (lambda i: i)

    def token_spec(cols, reverse):
        return pl.BlockSpec((part, 1, own, cols), lambda g, i: (at(reverse)(i), g, 0, 0))

    def before_spec(cols, reverse):
        return pl.BlockSpec(
            (1, 1, EDGE, cols),
            lambda g, i: (jnp.maximum(part * at(reverse)(i) - 1, 0), g, own // EDGE - 1, 0),
        )

    def group_spec(*dims):
        return pl.BlockSpec((1,) + dims, lambda g, i: (g,) + (0,) * len(dims))

    def whole_spec(*dims):
        return pl.BlockSpec(dims, lambda g, i: (0,) * len(dims))

    def kept_spec(reverse):
        return pl.BlockSpec((1, 1, STATE, width), lambda g, i: (g, at(reverse)(i), 0, 0))

    offs_spec = pl.BlockSpec(memory_space=pltpu.SMEM)

    def x_specs(reverse):
        return [token_spec(width, reverse), before_spec(width, reverse), group_spec(EDGE, width)]

    def s_specs(reverse):
        return [token_spec(SMALL, reverse), before_spec(SMALL, reverse), group_spec(EDGE, SMALL)]

    head_specs = [whole_spec(8, 128), whole_spec(128, 128), whole_spec(128, width)]
    x_args = (x_raw, x_raw, x_halo)
    s_args = (s_raw, s_raw, s_halo)
    head_args = (hp, pick, spread)
    state_ref = pltpu.VMEM((STATE, width), f32)
    fall_ref = pltpu.VMEM((8, width), f32)

    def call(kernel, in_specs, out_specs, out_shape, scratch, flops, moved):
        return pl.pallas_call(
            functools.partial(kernel, sequences),
            grid=(groups, chunks),
            in_specs=in_specs,
            out_specs=out_specs,
            out_shape=out_shape,
            scratch_shapes=scratch,
            compiler_params=pltpu.CompilerParams(
                dimension_semantics=("arbitrary", "arbitrary"), vmem_limit_bytes=VMEM_LIMIT
            ),
            cost_estimate=pl.CostEstimate(flops=flops, bytes_accessed=moved, transcendentals=0),
        )

    with jax.named_scope("memory_own"):
        ended = call(
            state_kernel,
            [offs_spec] + x_specs(False) + s_specs(False)
            + [whole_spec(8, width), whole_spec(8, MIX)] + head_specs,
            group_spec(STATE + EDGE, width),
            jax.ShapeDtypeStruct((groups, STATE + EDGE, width), bf16),
            [state_ref, fall_ref],
            4_000_000_000, 4_000_000,
        )(offsets, *x_args, *s_args, taps_x, taps_s, *head_args)
    ended_all = lax.all_gather(ended, "z", axis=0, tiled=False).astype(f32)
    falls = jnp.sum(ended_all[:, :, STATE : STATE + 3], axis=2, keepdims=True)
    incoming = jnp.zeros((groups, STATE, width), f32)
    for k in range(zn - 1):
        joined = falls[k] * incoming + ended_all[k, :, :STATE]
        incoming = jnp.where(k < z, joined, incoming)

    with jax.named_scope("scan"):
        scanned, kept = call(
            scan_kernel,
            [offs_spec] + x_specs(False) + s_specs(False)
            + [whole_spec(8, width), whole_spec(8, MIX)] + head_specs + [group_spec(STATE, width)],
            [token_spec(width, False), kept_spec(False)],
            [
                jax.ShapeDtypeStruct(token_shape + (width,), bf16),
                jax.ShapeDtypeStruct((groups, chunks, STATE, width), f32),
            ],
            [state_ref],
            8_000_000_000, 6_000_000,
        )(offsets, *x_args, *s_args, taps_x, taps_s, *head_args, incoming)

    gate_in = product(normed, w_z, 1, 0)
    grad_gnorm = product(cot_all, w_o, 1, 1)
    scan_b = scanned.reshape(tokens, width).astype(f32)
    gate_sig = jax.nn.sigmoid(gate_in)
    gate = gate_in * gate_sig
    gated = scan_b * gate
    grad_gain_in = grad_gnorm * gate_gain
    sums = jnp.stack([jnp.sum(gated * gated, axis=1), jnp.sum(grad_gain_in * gated, axis=1)])
    sums = lax.psum(sums, Q) / INNER
    inverse = lax.rsqrt(sums[0] + EPS)[:, None]
    gated_unit = gated * inverse
    gnorm = (gated_unit * gate_gain).astype(bf16)
    grad_gate_gain = jnp.sum(grad_gnorm * gated_unit, axis=0)
    grad_gated = inverse * (grad_gain_in - gated * (inverse * inverse * sums[1][:, None]))
    grad_scan = (grad_gated * gate).astype(bf16).reshape(token_shape + (width,))
    slope = gate_sig * (1.0 + gate_in * (1.0 - gate_sig))
    grad_z = (grad_gated * scan_b * slope).astype(bf16)

    branch = product(gnorm, w_o, 1, 0).astype(bf16).reshape(qn, groups, own, D)
    branch = lax.psum_scatter(branch, Q, scatter_dimension=0, tiled=False)
    result = (x_in.astype(f32) + branch.astype(f32)).astype(bf16)
    grad_out = product(gnorm, cot_all, 0, 0).astype(bf16)
    if strided:
        grad_out = lax.psum_scatter(grad_out, "z", scatter_dimension=0, tiled=True)
    else:
        full = jnp.zeros((INNER, D), bf16)
        full = lax.dynamic_update_slice_in_dim(full, grad_out, q * width, 0)
        grad_out = lax.psum_scatter(full, ALL, scatter_dimension=0, tiled=True)

    with jax.named_scope("memory_back"):
        direct = call(
            direct_kernel,
            [offs_spec] + s_specs(False) + [whole_spec(8, MIX)] + head_specs
            + [token_spec(width, False)],
            group_spec(STATE, width),
            jax.ShapeDtypeStruct((groups, STATE, width), bf16),
            [state_ref, fall_ref],
            2_000_000_000, 3_000_000,
        )(offsets, *s_args, taps_s, *head_args, grad_scan)
    direct_all = lax.all_gather(direct, "z", axis=0, tiled=False).astype(f32)
    later = jnp.zeros((groups, STATE, width), f32)
    for k in range(zn - 1, 0, -1):
        joined = falls[k] * later + direct_all[k]
        later = jnp.where(k > z, joined, later)

    def home(grad):
        cols = grad.shape[1]
        grad = grad.astype(bf16).reshape(zn, qn, rows_in, cols)
        grad = lax.psum_scatter(grad, "z", scatter_dimension=0, tiled=False)
        return lax.all_to_all(grad, Q, split_axis=0, concat_axis=0, tiled=True)

    home_z = home(product(normed, grad_z, 0, 0))

    with jax.named_scope("scan_back"):
        dx, ds, tail_x, tail_s, rim_x, rim_s, gx, gs, gh = call(
            back_kernel,
            [offs_spec] + x_specs(True) + s_specs(True)
            + [whole_spec(8, width), whole_spec(8, MIX)] + head_specs
            + [token_spec(width, True), kept_spec(True), group_spec(STATE, width)],
            [
                token_spec(width, True), token_spec(SMALL, True),
                group_spec(EDGE, width), group_spec(EDGE, MIX),
                group_spec(EDGE, width), group_spec(EDGE, MIX),
                whole_spec(8, width), whole_spec(8, MIX), whole_spec(8, 128),
            ],
            [
                jax.ShapeDtypeStruct(token_shape + (width,), bf16),
                jax.ShapeDtypeStruct(token_shape + (SMALL,), bf16),
                jax.ShapeDtypeStruct((groups, EDGE, width), f32),
                jax.ShapeDtypeStruct((groups, EDGE, MIX), f32),
                jax.ShapeDtypeStruct((groups, EDGE, width), f32),
                jax.ShapeDtypeStruct((groups, EDGE, MIX), f32),
                jax.ShapeDtypeStruct((8, width), f32),
                jax.ShapeDtypeStruct((8, MIX), f32),
                jax.ShapeDtypeStruct((8, 128), f32),
            ],
            [state_ref, pltpu.VMEM((8, width), f32), pltpu.VMEM((8, MIX), f32)],
            16_000_000_000, 9_000_000,
        )(offsets, *x_args, *s_args, taps_x, taps_s, *head_args, grad_scan, kept, later)
    rim_x, rim_s = shifted_along(rim_x, "z", -1), shifted_along(rim_s, "z", -1)
    dx = dx.at[qn - 1, :, own - EDGE :].set((tail_x + rim_x).astype(bf16))
    ds = ds.at[qn - 1, :, own - EDGE :, :MIX].set((tail_s + rim_s).astype(bf16))
    grad_x = dx.reshape(tokens, width)
    grad_s = ds.reshape(tokens, SMALL)

    home_x = home(product(normed, grad_x, 0, 0))
    home_s = home(product(normed, grad_s, 0, 0))
    grad_in = jnp.concatenate(
        [
            join(home_z, INNER),
            join(home_x, INNER),
            jnp.sum(home_s.astype(f32), axis=0)[:, : MIX + HEADS].astype(bf16),
        ],
        axis=1,
    ).astype(f32)

    grad_normed = (
        product(grad_z, w_z, 1, 1) + product(grad_x, w_x, 1, 1) + product(grad_s, w_small, 1, 1)
    )
    grad_norm_gain = jnp.sum(grad_normed * x_scaled, axis=0)
    grad_own = lax.psum_scatter(
        grad_normed.astype(bf16).reshape(qn, groups, own, D), Q, scatter_dimension=0, tiled=False
    ).astype(f32)
    x_own = x_in.astype(f32)
    inverse = lax.rsqrt(jnp.mean(x_own * x_own, axis=-1, keepdims=True) + EPS)
    grad_unit = grad_own * norm_gain
    pulled = jnp.mean(grad_unit * x_own, axis=-1, keepdims=True)
    grad_x_own = inverse * (grad_unit - x_own * (inverse * inverse * pulled))
    input_grad = (grad_x_own + cotangent.astype(f32)).astype(bf16)

    def place_own(array, size):
        mine = (jnp.arange(qn) == q).astype(f32).reshape((qn,) + (1,) * array.ndim)
        return join(array[None] * mine, size)

    table = jnp.concatenate([place_own(gx[:5], INNER), gs[:5]], axis=1)
    grad_vec = jnp.concatenate([grad_norm_gain, table[4], place_own(grad_gate_gain, INNER)])
    grad_skip = jnp.sum(gx[5].reshape(heads_own, HEAD_DIM), axis=1)
    grad_heads = jnp.concatenate([gh[:2, :heads_own], grad_skip[None]], axis=0)
    grad_heads = place_own(grad_heads, HEADS).reshape(3, head_size, head_cols)
    grad_heads = jnp.moveaxis(grad_heads, 1, 0).reshape(1, head_size, 3 * head_cols)
    grad_heads = jnp.broadcast_to(grad_heads, (devices // head_size,) + grad_heads.shape[1:])
    packed = jnp.concatenate(
        [
            jnp.moveaxis(table[:4].reshape(KW, devices, conv_rows), 1, 0).reshape(devices, -1),
            grad_vec.reshape(devices, vec_rows),
            grad_heads.reshape(devices, -1),
        ],
        axis=1,
    )
    used = packed.shape[1]
    packed = jnp.pad(packed, ((0, 0), (0, -used % 1024))).reshape(devices, -1, 128)
    packed = lax.psum_scatter(packed, ALL, scatter_dimension=0, tiled=False).reshape(-1)
    grad_conv = packed[: conv_rows * KW].reshape(KW, conv_rows).T
    grad_vec = packed[conv_rows * KW : conv_rows * KW + vec_rows]
    grad_head = packed[conv_rows * KW + vec_rows : used].reshape(3, head_cols)

    in_new = adam(w_in, m_in, v_in, grad_in, rate_input)
    out_new = adam(w_out, m_out, v_out, grad_out.astype(f32), rate_output)
    conv_new = adam(conv_w, m_conv, v_conv, grad_conv, rate_conv)
    vec_new = adam(vectors, m_vec, v_vec, grad_vec, rate_vector)
    head_new = adam(head_params, m_head, v_head, grad_head, rate_head)
    return (result, input_grad, *in_new, *out_new, *conv_new, *vec_new, *head_new)


def solution(mesh):
    seq, head = mesh.shape["seq"], mesh.shape["head"]
    fine = Mesh(mesh.devices.reshape(seq // 2, 2, head), ALL)
    token, row = P(None, ALL, None), P(ALL, None)
    line, heads = P(ALL), P(None, "head")
    return jax.shard_map(
        local,
        mesh=fine,
        in_specs=(token, P(), token) + (row,) * 9 + (line,) * 3 + (heads,) * 3,
        out_specs=(token, token) + (row,) * 9 + (line,) * 3 + (heads,) * 3,
        check_vma=False,
    )
```

time: 2190 us -> 856 us (0.39)
  waiting for transfers between devices: 1510 us -> 570 us
  blocking collectives: 220 us -> 42.6 us
  matrix products: 180 us -> 73.6 us
  local copies, waits for them, and re-layouts: 107 us -> 17 us
  other arithmetic: 119 us -> 38.7 us
  Pallas kernels: 0 us -> 69.2 us
    reduce_scatter x3 -> x6, waiting for transfers between devices: 1050 us -> 219 us  [the longest x3 85.3 us: home(): grad = lax.psum_scatter(grad, 'z', scatter_dimension=0, tiled=False)]
    all_gather x4 -> x8, waiting for transfers between devices: 355 us -> 228 us  [the longest x2 65.2 us: columns(): return lax.all_gather(mine, 'z', axis=0, tiled=False).reshape(D, width)]
    dot_general x22 -> x12, matrix products: 180 us -> 73.6 us  [product(): lax.dot_general(a, b, (((on_a,), (on_b,)), ((), ())), preferred_element_t...]
    unnamed x2 -> x0, blocking collectives: 93.1 us -> none
    all_gather x4 -> x0, blocking collectives: 86.2 us -> none  [the longest x1 41.9 us: local(): lax.all_gather(conv_w.astype(jnp.bfloat16), ('seq', 'head'), axis=0, tile...]
    pallas_call x0 -> x4, Pallas kernels: none -> 69.2 us  [the longest x1 32.4 us: local(): call(back_kernel, [offs_spec] + x_specs(True) + s_specs(True) + [whole_sp...]
    unnamed x9 -> x16, waiting for transfers between devices: 65.9 us -> 118 us
    all_to_all x5 -> x3, waiting for transfers between devices: 36.8 us -> 0.01 us  [home(): return lax.all_to_all(grad, Q, split_axis=0, concat_axis=0, tiled=True)]
  transfers between devices with their start and end apart: 15 -> 22, of which waited for: 11 -> 16; matrix products, arithmetic and copies ran while one was open for 6% -> 12% of each run, Pallas kernels for 0% -> 3%
where the time goes in v1:
time: 856 us; the launch traced here: 847 us
  waiting for transfers between devices  570 us (67%)
  matrix products  73.6 us (9%)
  Pallas kernels  69.2 us (8%)
  blocking collectives  42.6 us (5%)
  other arithmetic  38.7 us (5%)
  starting transfers between devices  20.6 us (2%)
  local copies, waits for them, and re-layouts  17 us (2%)
  between operations  15.4 us (2%)
    unnamed x16, waiting for transfers between devices  118 us
    reduce_scatter x3, waiting for transfers between devices, home(): grad = lax.psum_scatter(grad, 'z', scatter_dimension=0, tiled=False)  85.3 us
    dot_general x12, matrix products, product(): lax.dot_general(a, b, (((on_a,), (on_b,)), ((), ())), preferred_element_t...  73.6 us
    all_gather x2, waiting for transfers between devices, columns(): return lax.all_gather(mine, 'z', axis=0, tiled=False).reshape(D, width)  65.2 us
    reduce_scatter x1, waiting for transfers between devices, local(): branch = lax.psum_scatter(branch, Q, scatter_dimension=0, tiled=False)  53.1 us
    reduce_scatter x1, waiting for transfers between devices, local(): grad_out = lax.psum_scatter(grad_out, 'z', scatter_dimension=0, tiled=True)  42.5 us
    reduce_scatter x1, waiting for transfers between devices, local(): lax.psum_scatter(grad_normed.astype(bf16).reshape(qn, groups, own, D), Q,...  38.6 us
    all_gather x1, waiting for transfers between devices, local(): small_all = lax.all_gather(small_own, ALL, axis=0, tiled=False)  38.4 us
  transfers between devices with their start and end apart: 22, of which 16 were waited for; matrix products, arithmetic and copies ran while one was open for 12% of the time, Pallas kernels for 3%

profile of v1, /device:TPU:0, one launch (start us, length us, event | category | flops | bytes accessed | tf_op | source)
XLA Modules:
  0.0 847.4 jit_solution(2842134909536519183)
XLA Ops:
  14.4 15.2 %all_to_all.25 = bf16[8,64,512]{2,1,0:T(8,128)(2,1)} all-to-all(bf16[8,64,512]{2,1,0:T(8,128)(2,1)S(1)} %reshape.489), channel_id=1, replica_groups=mesh['z'=4,'y'=2,'head'=4] {'y','head'}, dimensions={0} | all-to-all | bytes 1048576 | tf_op jit(solution)/shard_map/all_to_all | solution.py:542
  31.7 38.4 %all-gather.20.cloned.1.call-done = bf16[2048,384]{1,0:T(8,128)(2,1)} async-done(((bf16[64,384]{1,0:T(8,128)(2,1)}), bf16[2048,384]{1,0:T(8,128)(2,1)}) %all-gather.20.cloned.1.call-update) | async-done | bytes 1572880 | tf_op jit(solution)/shard_map/all_gather | solution.py:511
  72.9 34.7 %all-gather.18.cloned.1.call-done = bf16[16,64,2048]{2,1,0:T(8,128)(2,1)} async-done(((bf16[2,64,2048]{2,1,0:T(8,128)(2,1)}), bf16[16,64,2048]{2,1,0:T(8,128)(2,1)}) %all-gather.18.cloned.1.call-update) | async-done | bytes 4194320 | tf_op jit(solution)/shard_map/all_gather | solution.py:537
  118.3 36.9 %all-gather.22.cloned.1.call-done = bf16[32,64,512]{2,1,0:T(8,128)(2,1)} async-done(((bf16[8,64,512]{2,1,0:T(8,128)(2,1)}), bf16[32,64,512]{2,1,0:T(8,128)(2,1)}) %all-gather.22.cloned.1.call-update) | async-done | bytes 2097168 | tf_op jit(solution)/shard_map/all_gather | solution.py:543
  163.8 12.2 %memory_own.1 = bf16[2,144,512]{2,1,0:T(8,128)(2,1)} custom-call(s32[2,3]{1,0:T(2,128)S(1)} %subtract_subtract_fusion.offs, bf16[8,2,64,512]{3,2,1,0:T(8,128)(2,1)S(1)} %bitcast.223, bf16[8,2,64,512]{3,2,1,0:T(8,128)(2,1)S(1)} %bitcast.224, bf16[2,16,512]{2,1,0:T(8,128)(2,1)S(1)} %collective-permute-done.xh, bf16[8,2,64,384]{3,2,1,0:T(8,128)(2,1)S(1)} %bitcast.230, ...), custom_call_target="tpu_custom_call" | custom-call | flops 4000000000 | bytes 4000000 | tf_op jit(solution)/shard_map/memory_own/pallas_call | solution.py:613
  176.6 13.5 %all_to_all.26 = bf16[8,64,512]{2,1,0:T(8,128)(2,1)} all-to-all(bf16[8,64,512]{2,1,0:T(8,128)(2,1)S(1)} %reshape.506), channel_id=1, replica_groups=mesh['z'=4,'y'=2,'head'=4] {'y','head'}, dimensions={0} | all-to-all | bytes 1048576 | tf_op jit(solution)/shard_map/all_to_all | solution.py:542
  190.7 11.9 %all-gather.16.cloned.1.call-done = bf16[512,2048]{1,0:T(8,128)(2,1)} async-done(((bf16[128,2048]{1,0:T(8,128)(2,1)}), bf16[512,2048]{1,0:T(8,128)(2,1)}) %all-gather.16.cloned.1.call-update) | async-done | bytes 2097168 | tf_op jit(solution)/shard_map/all_gather | solution.py:548
  202.6 37.2 %all-gather.28.cloned.1.call-done = bf16[16,64,2048]{2,1,0:T(8,128)(2,1)} async-done(((bf16[2,64,2048]{2,1,0:T(8,128)(2,1)}), bf16[16,64,2048]{2,1,0:T(8,128)(2,1)}) %all-gather.28.cloned.1.call-update) | async-done | bytes 4194320 | tf_op jit(solution)/shard_map/all_gather | solution.py:538
  246.3 25.9 %all-gather.24.cloned.1.call-done = bf16[8,144,512]{2,1,0:T(8,128)(2,1)} async-done(((bf16[2,144,512]{2,1,0:T(8,128)(2,1)}), bf16[8,144,512]{2,1,0:T(8,128)(2,1)}) %all-gather.24.cloned.1.call-update) | async-done | bytes 1179664 | tf_op jit(solution)/shard_map/all_gather | solution.py:622
  274.7 14.6 %scan.1 = (bf16[8,2,64,512]{3,2,1,0:T(8,128)(2,1)S(1)}, f32[2,4,128,512]{3,2,1,0:T(8,128)S(1)}) custom-call(s32[2,3]{1,0:T(2,128)S(1)} %subtract_subtract_fusion.offs, bf16[8,2,64,512]{3,2,1,0:T(8,128)(2,1)S(1)} %bitcast.225, bf16[8,2,64,512]{3,2,1,0:T(8,128)(2,1)S(1)} %bitcast.226, bf16[2,16,512]{2,1,0:T(8,128)(2,1)S(1)} %collective-permute-done.xh, ...), custom_call_target="tpu_custom_call" | custom-call | flops 8000000000 | bytes 6000000 | tf_op jit(solution)/shard_map/scan/pallas_call | solution.py:630
  290.6 28.3 %all-gather.26.cloned.1.call-done = bf16[32,64,512]{2,1,0:T(8,128)(2,1)} async-done(((bf16[8,64,512]{2,1,0:T(8,128)(2,1)}), bf16[32,64,512]{2,1,0:T(8,128)(2,1)}) %all-gather.26.cloned.1.call-update) | async-done | bytes 2097168 | tf_op jit(solution)/shard_map/all_gather | solution.py:543
  318.9 7.6 multiply_reduce_fusion.4
  326.5 14.0 %psum.7 = f32[2,1024]{1,0:T(2,128)S(1)} all-reduce(f32[2,1024]{1,0:T(2,128)S(1)} %pad_maximum_fusion.4), channel_id=1, replica_groups=mesh['z'=4,'y'=2,'head'=4] {'y','head'}, use_global_device_ids=true, to_apply=%region_7.8 | all-reduce | flops 2048 | bytes 16384 | tf_op jit(solution)/shard_map/psum | solution.py:651
  345.7 10.1 %memory_back.1 = bf16[2,128,512]{2,1,0:T(8,128)(2,1)} custom-call(s32[2,3]{1,0:T(2,128)S(1)} %subtract_subtract_fusion.offs, bf16[8,2,64,384]{3,2,1,0:T(8,128)(2,1)S(1)} %bitcast.234, bf16[8,2,64,384]{3,2,1,0:T(8,128)(2,1)S(1)} %bitcast.235, bf16[2,16,384]{2,1,0:T(8,128)(2,1)S(1)} %collective-permute-done.1.sh, f32[8,256]{1,0:T(8,128)S(1)} %slice.238.ts, ...), custom_call_target="tpu_custom_call" | custom-call | flops 2000000000 | bytes 3000000 | tf_op jit(solution)/shard_map/memory_back/pallas_call | solution.py:673
  366.1 14.8 %all-gather.30.cloned.1.call-done = bf16[8,128,512]{2,1,0:T(8,128)(2,1)} async-done(((bf16[2,128,512]{2,1,0:T(8,128)(2,1)}), bf16[8,128,512]{2,1,0:T(8,128)(2,1)}) %all-gather.30.cloned.1.call-update) | async-done | bytes 1048592 | tf_op jit(solution)/shard_map/all_gather | solution.py:682
  382.7 32.4 %scan_back.1 = (bf16[8,2,64,512]{3,2,1,0:T(8,128)(2,1)S(1)}, bf16[8,2,64,384]{3,2,1,0:T(8,128)(2,1)S(1)}, f32[2,16,512]{2,1,0:T(8,128)S(1)}, f32[2,16,256]{2,1,0...) custom-call(s32[2,3]{1,0:T(2,128)S(1)} %subtract_subtract_fusion.off, ...), custom_call_target="tpu_custom_call" | custom-call | flops 16000000000 | bytes 9000000 | tf_op jit(solution)/shard_map/scan_back/pallas_call | solution.py:697
  436.7 9.4 %multiply_reduce_fusion = (f32[2048]{0:T(1024)S(1)}, bf16[1024,2048]{1,0:T(8,128)(2,1)}, bf16[1024,2048]{1,0:T(8,128)(2,1)}) fusion(bf16[16,64,2048]{2,1,0:T(8,128)(2,1)S(1)} %copy-done.7, f32[1024]{0:T(1024)S(1)} %copy-done.27, f32[2048]{0:T(1024)S(1)} %slice.231, bf16[1024,384]{1,0:T(8,128)(2,1)S(1)} %bitcast.218, bf16[2048,384]{1,0:T(8,128)(2,1)S(1)} %copy-done.14, ...), kind=kOutput, calls=%fused_computation.1 | convolution fusion | flops 1629485056 | bytes 31739904 | tf_op jit(solution)/shard_map/dot_general | solution.py:457
  475.0 116.1 %all-reduce.7.cloned.1.call-done = f32[32,8,128]{2,1,0:T(8,128)} async-done(((f32[32,8,128]{2,1,0:T(8,128)}), f32[32,8,128]{2,1,0:T(8,128)}) %all-reduce.7.cloned.1.call-update) | async-done | bytes 131088
  591.9 45.0 %reduce-scatter.13.cloned.1.call-done = bf16[1,8,64,512]{3,2,1,0:T(8,128)(2,1)} async-done(((bf16[4,8,64,512]{3,2,1,0:T(8,128)(2,1)}), bf16[1,8,64,512]{3,2,1,0:T(8,128)(2,1)}) %reduce-scatter.13.cloned.1.call-update) | async-done | bytes 524304 | tf_op jit(solution)/shard_map/reduce_scatter | solution.py:691
  642.6 40.3 %reduce-scatter.11.cloned.1.call-done = bf16[1,8,64,512]{3,2,1,0:T(8,128)(2,1)} async-done(((bf16[4,8,64,512]{3,2,1,0:T(8,128)(2,1)}), bf16[1,8,64,512]{3,2,1,0:T(8,128)(2,1)}) %reduce-scatter.11.cloned.1.call-update) | async-done | bytes 524304 | tf_op jit(solution)/shard_map/reduce_scatter | solution.py:691
  686.6 42.5 %reduce-scatter.17.cloned.1.call-done = bf16[128,2048]{1,0:T(8,128)(2,1)} async-done(((bf16[512,2048]{1,0:T(8,128)(2,1)}), bf16[128,2048]{1,0:T(8,128)(2,1)}) %reduce-scatter.17.cloned.1.call-update) | async-done | bytes 524304 | tf_op jit(solution)/shard_map/reduce_scatter | solution.py:666
  737.2 7.5 multiply_subtract_fusion
  744.7 38.6 %reduce-scatter.9.cloned.1.call-done = bf16[1,2,64,2048]{3,2,1,0:T(8,128)(2,1)} async-done(((bf16[8,2,64,2048]{3,2,1,0:T(8,128)(2,1)}), bf16[1,2,64,2048]{3,2,1,0:T(8,128)(2,1)}) %reduce-scatter.9.cloned.1.call-update) | async-done | bytes 524304 | tf_op jit(solution)/shard_map/reduce_scatter | solution.py:743
  784.6 53.1 %reduce-scatter.7.cloned.1.call-done = bf16[1,2,64,2048]{3,2,1,0:T(8,128)(2,1)} async-done(((bf16[8,2,64,2048]{3,2,1,0:T(8,128)(2,1)}), bf16[1,2,64,2048]{3,2,1,0:T(8,128)(2,1)}) %reduce-scatter.7.cloned.1.call-update) | async-done | bytes 524304 | tf_op jit(solution)/shard_map/reduce_scatter | solution.py:662
  (259 shorter events, 132.0 us)
Async XLA Ops:
  7.2 62.9 %all-gather.20.cloned.1.call-start = ((), (), s32[]{:S(2)}) async-start(), calls=%async_computation.19 | async-start | bytes 1622016 | tf_op jit(solution)/shard_map/all_gather | solution.py:511
  12.1 95.5 %all-gather.18.cloned.1.call-start = ((), (), s32[]{:S(2)}) async-start(), calls=%async_computation.18 | async-start | bytes 4718592 | tf_op jit(solution)/shard_map/all_gather | solution.py:537
  12.9 142.3 %all-gather.22.cloned.1.call-start = ((), (), s32[]{:S(2)}) async-start(), calls=%async_computation.20 | async-start | bytes 2621440 | tf_op jit(solution)/shard_map/all_gather | solution.py:543
  29.6 173.0 %all-gather.16.cloned.1.call-start = ((), (), s32[]{:S(2)}) async-start(), calls=%async_computation.11 | async-start | bytes 2621440 | tf_op jit(solution)/shard_map/all_gather | solution.py:548
  30.5 209.3 %all-gather.28.cloned.1.call-start = ((), (), s32[]{:S(2)}) async-start(), calls=%async_computation.23 | async-start | bytes 4718592 | tf_op jit(solution)/shard_map/all_gather | solution.py:538
  31.1 241.2 %all-gather.24.cloned.1.call-start = ((), (), s32[]{:S(2)}) async-start(), calls=%async_computation.21 | async-start | bytes 1474560 | tf_op jit(solution)/shard_map/all_gather | solution.py:622
  114.9 47.4 %collective-permute-start.1 = (bf16[2,16,384]{2,1,0:T(8,128)(2,1)S(1)}, bf16[2,16,384]{2,1,0:T(8,128)(2,1)S(1)}, u32[]{:S(2)}, u32[]{:S(2)}) collective-permute-start(bf16[2,16,384]{2,1,0:T(8,128)(2,1)S(1)} %slice_bitcast_fusion.6), channel_id=1, source_target_pairs={{0,8},{8,16},{16,24},{1,9},{9,17},{17,25},{2,10},{10,18},{18,26},{... | collective-permute-start | bytes 73736 | tf_op jit(solution)/shard_map/ppermute | solution.py:446
  160.4 3.4 collective-permute-start
  176.0 142.9 %all-gather.26.cloned.1.call-start = ((), (), s32[]{:S(2)}) async-start(), calls=%async_computation.22 | async-start | bytes 2621440 | tf_op jit(solution)/shard_map/all_gather | solution.py:543
  190.1 190.8 %all-gather.30.cloned.1.call-start = ((), (), s32[]{:S(2)}) async-start(), calls=%async_computation.24 | async-start | bytes 1310720 | tf_op jit(solution)/shard_map/all_gather | solution.py:682
  355.8 115.4 %reduce-scatter.15.cloned.1.call-start = ((), (), s32[]{:S(2)}) async-start(), calls=%async_computation.16 | async-start | bytes 1966080 | tf_op jit(solution)/shard_map/reduce_scatter | solution.py:691
  416.5 5.8 collective-permute-start.3
  417.9 11.2 %collective-permute-start.2 = (f32[2,16,512]{2,1,0:T(8,128)S(1)}, f32[2,16,512]{2,1,0:T(8,128)S(1)}, u32[]{:S(2)}, u32[]{:S(2)}) collective-permute-start(f32[2,16,512]{2,1,0:T(8,128)S(1)} %get-tuple-element.56), channel_id=1, source_target_pairs={{8,0},{16,8},{24,16},{9,1},{17,9},{25,17},{10,2},{18,10},{26,18},{... | collective-permute-start | bytes 196616 | tf_op jit(solution)/shard_map/ppermute | solution.py:446
  428.1 163.0 %all-reduce.7.cloned.1.call-start = ((), (), s32[]{:S(2)}) async-start(), calls=%async_computation.25 | async-start | bytes 262144
  447.1 189.8 %reduce-scatter.13.cloned.1.call-start = ((), (), s32[]{:S(2)}) async-start(), calls=%async_computation.15 | async-start | bytes 2621440 | tf_op jit(solution)/shard_map/reduce_scatter | solution.py:691
  453.1 229.8 %reduce-scatter.11.cloned.1.call-start = ((), (), s32[]{:S(2)}) async-start(), calls=%async_computation.14 | async-start | bytes 2621440 | tf_op jit(solution)/shard_map/reduce_scatter | solution.py:691
  459.2 269.8 %reduce-scatter.17.cloned.1.call-start = ((), (), s32[]{:S(2)}) async-start(), calls=%async_computation.17 | async-start | bytes 2621440 | tf_op jit(solution)/shard_map/reduce_scatter | solution.py:666
  465.2 318.1 %reduce-scatter.9.cloned.1.call-start = ((), (), s32[]{:S(2)}) async-start(), calls=%async_computation.13 | async-start | bytes 4718592 | tf_op jit(solution)/shard_map/reduce_scatter | solution.py:743
  465.7 372.0 %reduce-scatter.7.cloned.1.call-start = ((), (), s32[]{:S(2)}) async-start(), calls=%async_computation.12 | async-start | bytes 4718592 | tf_op jit(solution)/shard_map/reduce_scatter | solution.py:662
  471.1 170.8 %copy-start.26 = (f32[136,4]{0,1:T(4,128)S(1)}, f32[136,4]{0,1:T(4,128)}, u32[]{:S(2)}) copy-start(f32[136,4]{0,1:T(4,128)} %param.31) | copy-start | bytes 6532
  471.1 257.9 %copy-start.12 = (f32[128,2048]{1,0:T(8,128)S(1)}, f32[128,2048]{1,0:T(8,128)}, u32[]{:S(2)}) copy-start(f32[128,2048]{1,0:T(8,128)} %param.28) | copy-start | bytes 3145732
  471.2 120.7 %all-to-all-start.4 = ((bf16[8,64,384]{2,1,0:T(8,128)(2,1)}), bf16[8,64,384]{2,1,0:T(8,128)(2,1)S(1)}, u32[]{:S(2)}, u32[]{:S(2)}) async-start(bf16[8,64,384]{2,1,0:T(8,128)(2,1)} %bitcast.261), calls=%async_computation.9 | async-start | bytes 786432 | tf_op jit(solution)/shard_map/all_to_all | solution.py:692
  636.9 46.0 %all-to-all-start.3 = ((bf16[8,64,512]{2,1,0:T(8,128)(2,1)}), bf16[8,64,512]{2,1,0:T(8,128)(2,1)S(1)}, u32[]{:S(2)}, u32[]{:S(2)}) async-start(bf16[8,64,512]{2,1,0:T(8,128)(2,1)} %bitcast.256), calls=%async_computation.7 | async-start | bytes 1048576 | tf_op jit(solution)/shard_map/all_to_all | solution.py:692
  682.9 52.1 %all-to-all-start.2 = ((bf16[8,64,512]{2,1,0:T(8,128)(2,1)}), bf16[8,64,512]{2,1,0:T(8,128)(2,1)S(1)}, u32[]{:S(2)}, u32[]{:S(2)}) async-start(bf16[8,64,512]{2,1,0:T(8,128)(2,1)} %bitcast.255), calls=%async_computation.5 | async-start | bytes 1048576 | tf_op jit(solution)/shard_map/all_to_all | solution.py:692
  (38 other events, 1875.8 us)
Sparse Core Ops, SparseCore 0:
  12.3 57.8 all-gather.19
  72.0 35.5 all-gather.17
  109.2 45.9 all-gather.21
  157.2 45.3 all-gather.15
  204.3 35.4 all-gather.27
  241.8 30.4 all-gather.23
  273.8 45.0 all-gather.25
  355.9 24.9 all-gather.29
  428.2 35.4 reduce-scatter.14
  469.6 121.4 all-reduce.6
  593.9 42.8 reduce-scatter.12
  639.7 43.1 reduce-scatter.10
  685.8 43.1 reduce-scatter.16
  732.6 50.6 reduce-scatter.8
  786.5 51.2 reduce-scatter.6

commit v2 on v1

--- a/solution.py
+++ b/solution.py
@@ -34,9 +34,14 @@
 HIGH = lax.Precision.HIGHEST
 f32 = jnp.float32
 bf16 = jnp.bfloat16
-Q = ("y", "head")
-ALL = ("z", "y", "head")
+ROW = ("zh", "y")
+Q = ("zl", "x", "core")
+ALL = ("zh", "zl", "y", "x", "core")
 VMEM_LIMIT = 48 * 1024 * 1024
+
+
+def cost(us):
+    return pl.CostEstimate(flops=int(us * 0.4e9), bytes_accessed=1000, transcendentals=0)
 
 
 def dot(a, b, on_a=1, on_b=0):
@@ -45,14 +50,30 @@
     )
 
 
-def dot_exact(a, b, on_a=1, on_b=0):
-    return lax.dot_general(
-        a, b, (((on_a,), (on_b,)), ((), ())), preferred_element_type=f32, precision=HIGH
-    )
+def split_two(value):
+    high = value.astype(bf16)
+    return high, (value - high.astype(f32)).astype(bf16)
+
+
+def widen(value, spread):
+    return dot(jnp.concatenate(split_two(value), axis=1), spread)
+
+
+def narrow(value, spread):
+    high, low = split_two(value)
+    ones = spread[:128]
+    return dot(high, ones, 1, 1) + dot(low, ones, 1, 1)
+
+
+def running_sum(lower, value, on=1):
+    high, middle = split_two(value)
+    low = (value - high.astype(f32) - middle.astype(f32)).astype(bf16)
+    parts = jnp.concatenate([high, middle, low], axis=0)
+    return dot(jnp.concatenate([lower] * 3, axis=on), parts, on, 0)
 
 
 def sigmoid(v):
-    return 1.0 / (1.0 + jnp.exp(-v))
+    return 0.5 * jnp.tanh(0.5 * v) + 0.5
 
 
 def softplus(v):
@@ -119,8 +140,18 @@
         lax.broadcasted_iota(jnp.int32, (CHUNK, CHUNK), 0)
         >= lax.broadcasted_iota(jnp.int32, (CHUNK, CHUNK), 1)
     ).astype(f32)
-    running = dot_exact(lower, log_a)
+    running = running_sum(lower, log_a)
     return shifted, step, log_a, running, lower
+
+
+def pack(out, memory, fall):
+    high = fall.astype(bf16)
+    middle = (fall - high.astype(f32)).astype(bf16)
+    low = (fall - high.astype(f32) - middle.astype(f32)).astype(bf16)
+    out[0, :STATE] = memory.astype(bf16)
+    out[0, STATE:] = jnp.concatenate(
+        [high, middle, low, jnp.zeros((EDGE - 3, high.shape[1]), bf16)], axis=0
+    )
 
 
 def state_kernel(sequences, offs, x, xp, xh, s, sp, sh, tx, ts, hp, pick, spread, out, carry, fall):
@@ -144,21 +175,15 @@
     _, step, _, running, _ = steps_of(small, pick[...], hp[...])
     end = running[CHUNK - 1 : CHUNK]
     weight = jnp.exp(end - running) * place.open_end * step
-    carried = dot_exact(jnp.broadcast_to(jnp.exp(end) * place.unbroken, (8, 128)), spread[...])[0:1]
-    memory = carried * carry[...] + dot(keys, values * dot_exact(weight, spread[...]), 0, 0)
+    carried = widen(jnp.broadcast_to(jnp.exp(end) * place.unbroken, (8, 128)), spread[...])[0:1]
+    memory = carried * carry[...] + dot(keys, values * widen(weight, spread[...]), 0, 0)
     total = fall[0:1] * carried
     carry[...] = memory
     fall[...] = jnp.broadcast_to(total, fall.shape)
 
     @pl.when(chunk == pl.num_programs(1) - 1)
     def _():
-        high = total.astype(bf16)
-        middle = (total - high.astype(f32)).astype(bf16)
-        low = (total - high.astype(f32) - middle.astype(f32)).astype(bf16)
-        out[0, :STATE] = memory.astype(bf16)
-        out[0, STATE:] = jnp.concatenate(
-            [high, middle, low, jnp.zeros((EDGE - 3, high.shape[1]), bf16)], axis=0
-        )
+        pack(out, memory, total)
 
 
 def scan_kernel(sequences, offs, x, xp, xh, s, sp, sh, tx, ts, hp, pick, spread, first, out, kept, carry):
@@ -186,7 +211,7 @@
     inflow = jnp.exp(running) * place.fresh
     weight = jnp.exp(end - running) * place.open_end
     carried = jnp.exp(end) * place.unbroken
-    wide = dot_exact(
+    wide = widen(
         jnp.concatenate([step, inflow, weight, jnp.broadcast_to(carried, (8, 128)), hp[...]], axis=0),
         spread[...],
     )
@@ -228,7 +253,7 @@
     queries = act_c * sigmoid(act_c)
     _, _, _, running, _ = steps_of(small, pick[...], hp[...])
     end = running[CHUNK - 1 : CHUNK]
-    wide = dot_exact(
+    wide = widen(
         jnp.concatenate(
             [
                 jnp.exp(running) * place.fresh,
@@ -241,11 +266,12 @@
     grad = rows_of(dy).astype(f32) * wide[:CHUNK]
     total = carry[...] + fall[0:1] * dot(queries, grad, 0, 0)
     carry[...] = total
-    fall[...] = fall[...] * wide[CHUNK : CHUNK + 1]
+    falls = fall[0:1] * wide[CHUNK : CHUNK + 1]
+    fall[...] = jnp.broadcast_to(falls, fall.shape)
 
     @pl.when(chunk == pl.num_programs(1) - 1)
     def _():
-        out[0] = total.astype(bf16)
+        pack(out, total, falls)
 
 
 def conv_back(du, ahead, taps, own_seg, ahead_segs):
@@ -277,7 +303,7 @@
 
 def back_kernel(
     sequences, offs, x, xp, xh, s, sp, sh, tx, ts, hp, pick, spread, dy, kept, later,
-    dx, ds, tail_x, tail_s, rim_x, rim_s, gx, gs, gh, carry, next_x, next_s,
+    dx, tail, rim, gx, gs, gh, carry, next_x, next_s,
 ):
     group = pl.program_id(0)
     chunks = pl.num_programs(1)
@@ -317,7 +343,7 @@
     shifted, step, log_a, running, lower = steps_of(small, pick[...], hp[...])
     end = running[CHUNK - 1 : CHUNK]
     carried = jnp.exp(end) * place.unbroken
-    wide = dot_exact(
+    wide = widen(
         jnp.concatenate(
             [
                 step,
@@ -384,17 +410,15 @@
     )
     carry[...] = carried_w * back + dot(queries, grad_in, 0, 0)
 
-    narrow = dot_exact(
+    sums = narrow(
         jnp.concatenate(
             [grad_run, back_weighted * values, jnp.broadcast_to(end_sum, (8, width))], axis=0
         ),
         spread[...],
-        1,
-        1,
-    )
-    grad_log = dot_exact(lower, run_cols + narrow[:CHUNK], 0, 0) + narrow[2 * CHUNK : 2 * CHUNK + 1]
+    )
+    grad_log = running_sum(lower, run_cols + sums[:CHUNK], 0) + sums[2 * CHUNK : 2 * CHUNK + 1]
     rate = -jnp.exp(hp[1:2])
-    grad_step = (narrow[CHUNK : 2 * CHUNK] + grad_log * rate) * sigmoid(shifted)
+    grad_step = (sums[CHUNK : 2 * CHUNK] + grad_log * rate) * sigmoid(shifted)
     gh[0:1] += jnp.sum(grad_step, axis=0, keepdims=True)
     gh[1:2] += jnp.sum(grad_log * log_a, axis=0, keepdims=True)
 
@@ -413,20 +437,65 @@
     next_x[...] = du_x[:8]
     next_s[...] = du_m[:8]
     shape = (dx.shape[0], dx.shape[2])
-    dx[:, 0] = grad_x.astype(bf16).reshape(shape + (width,))
-    ds[:, 0, :, :MIX] = grad_m.astype(bf16).reshape(shape + (MIX,))
+    dx[:, 0, :, :width] = grad_x.astype(bf16).reshape(shape + (width,))
+    dx[:, 0, :, width : width + MIX] = grad_m.astype(bf16).reshape(shape + (MIX,))
     placed = dot(grad_step, pick[...], 1, 1)
-    ds[:, 0, :, MIX:] = placed.astype(bf16).reshape(shape + (SMALL - MIX,))
+    dx[:, 0, :, width + MIX :] = placed.astype(bf16).reshape(shape + (SMALL - MIX,))
 
     @pl.when(chunk == chunks - 1)
     def _():
-        tail_x[0] = grad_x[CHUNK - EDGE :]
-        tail_s[0] = grad_m[CHUNK - EDGE :]
+        tail[0, :, :width] = grad_x[CHUNK - EDGE :]
+        tail[0, :, width:] = grad_m[CHUNK - EDGE :]
 
     @pl.when(chunk == 0)
     def _():
-        rim_x[0] = conv_rim(du_x, tx[...], seg)
-        rim_s[0] = conv_rim(du_m, ts[...], seg)
+        rim[0, :, :width] = conv_rim(du_x, tx[...], seg)
+        rim[0, :, width:] = conv_rim(du_m, ts[...], seg)
+
+
+def back_projection_kernel(gz, gx, wz, wx, ws, x, out, sums):
+    width = wx.shape[1]
+    grad = dot(gz[...], wz[...], 1, 1) + dot(gx[:, :width], wx[...], 1, 1)
+    grad = grad + dot(gx[:, width:], ws[...], 1, 1)
+    out[...] = grad.astype(bf16)
+    rows = x[...].astype(f32)
+    unit = rows * lax.rsqrt(jnp.mean(rows * rows, axis=1, keepdims=True) + EPS)
+    partial = (grad * unit).reshape(-1, 8, D)
+
+    @pl.when(pl.program_id(0) == 0)
+    def _():
+        sums[...] = jnp.zeros_like(sums)
+
+    sums[...] += jnp.sum(partial, axis=0)
+
+
+def back_projection(grads, weights, x_all, deps):
+    tokens = x_all.shape[0]
+    block = 256
+
+    def rows(cols):
+        return pl.BlockSpec((block, cols), lambda i: (i, 0))
+
+    def kernel(*refs):
+        back_projection_kernel(*refs[:6], *refs[6 + len(deps) :])
+
+    return pl.pallas_call(
+        kernel,
+        grid=(tokens // block,),
+        in_specs=[rows(grad.shape[1]) for grad in grads]
+        + [pl.BlockSpec(w.shape, lambda i: (0, 0)) for w in weights]
+        + [rows(D)]
+        + [pl.BlockSpec(memory_space=pl.ANY)] * len(deps),
+        out_specs=[rows(D), pl.BlockSpec((8, D), lambda i: (0, 0))],
+        out_shape=[
+            jax.ShapeDtypeStruct((tokens, D), bf16),
+            jax.ShapeDtypeStruct((8, D), f32),
+        ],
+        compiler_params=pltpu.CompilerParams(
+            dimension_semantics=("arbitrary",), vmem_limit_bytes=VMEM_LIMIT
+        ),
+        cost_estimate=cost(0),
+    )(*grads, *weights, x_all, *deps)
 
 
 def adam(weight, first, second, grad, rate):
@@ -446,6 +515,312 @@
     return lax.ppermute(value, axis, pairs)
 
 
+def adam_kernel(last, refs):
+    home, small, weight, first, second, *outs = refs
+    cuts = range(0, home.shape[2], 128)
+    grad = [home[k, :, cut : cut + 128] for cut in cuts for k in range(home.shape[0])]
+    grad = jnp.concatenate(grad, axis=1).astype(f32)
+    if last:
+        extra = jnp.zeros((grad.shape[0], grad.shape[1] - SMALL), f32)
+        extra = jnp.concatenate([small[...], extra], axis=1)
+        grad = jnp.where(pl.program_id(0) == last, extra, grad)
+    new = adam(weight[...], first[...], second[...], grad, rate_input)
+    for out, value in zip(outs[-3:], new):
+        out[...] = value
+
+
+def adam_columns(state, home, small, start, done):
+    senders, rows, width = home.shape
+    steps = 4
+    block = pl.BlockSpec((rows, senders * 128), lambda i: (0, start + i))
+
+    def sent(i):
+        i = jnp.minimum(i, steps - 1)
+        return (lax.rem(i, 2), 0, lax.div(i, 2))
+
+    specs = [pl.BlockSpec((senders // 2, rows, width // 2), sent)]
+    args = [home]
+    if small is not None:
+        specs.append(pl.BlockSpec(small.shape, lambda i: (0, 0)))
+        args.append(small)
+    specs += [block] * 3
+    args += state
+    aliases = {}
+    if done is not None:
+        aliases = {len(args) + k: k for k in range(3)}
+        specs += [pl.BlockSpec(memory_space=pl.ANY)] * 3
+        args += done
+
+    def kernel(*refs):
+        refs = list(refs)
+        if small is None:
+            refs.insert(1, None)
+        adam_kernel(0 if small is None else steps, refs)
+
+    return pl.pallas_call(
+        kernel,
+        grid=(steps + (small is not None),),
+        in_specs=specs,
+        out_specs=[block] * 3,
+        out_shape=[jax.ShapeDtypeStruct(part.shape, f32) for part in state],
+        input_output_aliases=aliases,
+        compiler_params=pltpu.CompilerParams(
+            dimension_semantics=("arbitrary",), vmem_limit_bytes=VMEM_LIMIT
+        ),
+        cost_estimate=pl.CostEstimate(flops=0, bytes_accessed=1000, transcendentals=0),
+    )(*args)
+
+
+def halo_before(value):
+    size = lax.axis_size("y")
+    zh, y = lax.axis_index("zh"), lax.axis_index("y")
+    near = lax.ppermute(value, "y", [(i, (i + 1) % size) for i in range(size)])
+    far = lax.ppermute(value[1], ROW, [(size - 1, size)])
+    wrapped = jnp.stack([far, near[0]])
+    return jnp.where(y > 0, near, wrapped)
+
+
+def halo_after(value):
+    size = lax.axis_size("y")
+    y = lax.axis_index("y")
+    near = lax.ppermute(value, "y", [((i + 1) % size, i) for i in range(size)])
+    far = lax.ppermute(value[0], ROW, [(size, size - 1)])
+    wrapped = jnp.stack([near[1], far])
+    return jnp.where(y < size - 1, near, wrapped)
+
+
+def passed(value, reverse, first=(), second=(), started=None):
+    size = lax.axis_size("y")
+    zh, y = lax.axis_index("zh"), lax.axis_index("y")
+    others = [value]
+    for far in range(1, size):
+        others.append(lax.ppermute(value, "y", [(i, (i + far) % size) for i in range(size)]))
+
+    def fold(memory, order, found):
+        for zl, at in order:
+            found[zl] = jnp.where(y == at, memory, found[zl])
+            packed = others[0][zl]
+            for far in range(1, size):
+                packed = jnp.where(lax.rem(y - at + size, size) == far, others[far][zl], packed)
+            memory = carried_over(memory, packed)
+        return memory
+
+    order = [(zl, at) for zl in range(2) for at in range(size)]
+    order = order[::-1] if reverse else order
+    shape = value.shape[1:2] + (STATE,) + value.shape[3:]
+    zeros = jnp.zeros(shape, f32)
+    others[1] = after(others[1], *first)
+    extra = started(others[1]) if started else None
+    half = fold(zeros, order, [zeros, zeros]).astype(bf16)
+    half = lax.ppermute(half, "zh", [(1, 0)] if reverse else [(0, 1)])
+    half = after(half, *second, extra).astype(f32)
+    found = [zeros, zeros]
+    fold(half, order, found)
+    return jnp.concatenate(found, axis=0), others[1], extra
+
+
+def swapped(value, axis):
+    return lax.ppermute(value, axis, [(0, 1), (1, 0)])
+
+
+def is_square(axes):
+    return [lax.axis_size(axis) for axis in axes] == [2] * len(axes)
+
+
+def flip(axis):
+    return lax.axis_index(axis), 1 - lax.axis_index(axis)
+
+
+def gather_q(value, deps=(), deps_corner=()):
+    from_x, from_z = swapped(value, "x"), swapped(value, "zl")
+    from_z = after(from_z, *deps)
+    corner = after(swapped(from_z, "x"), *deps_corner)
+    z, x, core = (lax.axis_index(axis) for axis in Q)
+    places, pieces = [], []
+    for dz, dx, block in ((0, 0, value), (0, 1, from_x), (1, 0, from_z), (1, 1, corner)):
+        place = ((z ^ dz) * 2 + (x ^ dx)) * 2
+        for other in (0, 1):
+            places.append(place + (core ^ other))
+            pieces.append(swapped(block, "core") if other else block)
+    return jnp.stack(places).astype(jnp.int32), pieces
+
+
+def gather_row(value):
+    from_y, from_z = swapped(value, "y"), swapped(value, "zh")
+    corner = swapped(from_z, "y")
+    zh, y = lax.axis_index("zh"), lax.axis_index("y")
+    bits = [(zh ^ dz, y ^ dy) for dz in (0, 1) for dy in (0, 1)]
+    return (bits, [value, from_y, from_z, corner]), (from_y, from_z)
+
+
+def front_kernel(places, *refs):
+    pieces, rows_of_w, gain = refs[:8], refs[8:12], refs[12]
+    x_out, normed_out, small_out, w_out = refs[13:]
+    step = pl.program_id(0)
+    for k in range(8):
+
+        @pl.when(step == k)
+        def _(piece=pieces[k], w=rows_of_w[k // 2], part=k % 2):
+            rows = piece[...]
+            kept = x_out.shape[1]
+            x_out[0] = rows[:kept]
+            packed_rows(rows[kept:], small_out)
+            rows = rows[:kept].astype(f32)
+            inverse = lax.rsqrt(jnp.mean(rows * rows, axis=1, keepdims=True) + EPS)
+            normed_out[0] = (rows * inverse * gain[...]).astype(bf16)
+            size = w_out.shape[1]
+            w_out[0] = w[part * size : part * size + size]
+
+
+def front(tokens_gathered, w_gathered, gain, kept, row_count):
+    spots, pieces = tokens_gathered
+    bits, blocks = w_gathered
+    w_spots = [(zh * 2 + zl) * 2 + y for zh, y in bits for zl in (0, 1)]
+    places = jnp.stack([spots, jnp.stack(w_spots).astype(jnp.int32)])
+    rows, cols = pieces[0].shape
+    w_rows, width = blocks[0].shape
+    shapes = [(8, kept, cols)] * 2 + [(8, row_count, D // 32, SMALL), (8, w_rows // 2, width)]
+
+    def out_spec(shape, line):
+        tail = (0,) * (len(shape) - 1)
+        return pl.BlockSpec((1,) + shape[1:], lambda i, at: (at[line, i],) + tail)
+
+    return pl.pallas_call(
+        front_kernel,
+        grid_spec=pltpu.PrefetchScalarGridSpec(
+            num_scalar_prefetch=1,
+            grid=(8,),
+            in_specs=[pl.BlockSpec((rows, cols), lambda i, at: (0, 0))] * 8
+            + [pl.BlockSpec((w_rows, width), lambda i, at: (0, 0))] * 4
+            + [pl.BlockSpec((1, cols), lambda i, at: (0, 0))],
+            out_specs=[out_spec(shape, k // 3) for k, shape in enumerate(shapes)],
+        ),
+        out_shape=[jax.ShapeDtypeStruct(shape, bf16) for shape in shapes],
+        compiler_params=pltpu.CompilerParams(
+            dimension_semantics=("arbitrary",), vmem_limit_bytes=VMEM_LIMIT
+        ),
+        cost_estimate=cost(0),
+    )(places, *pieces, *blocks, gain[None])
+
+
+def late_kernel(places, *refs):
+    wz, wo, z_out, o_out = refs[:4], refs[4:8], refs[8], refs[9]
+    for k in range(4):
+
+        @pl.when(pl.program_id(0) == k)
+        def _(z=wz[k], o=wo[k]):
+            z_out[0, :, 0] = z[...].reshape(z_out.shape[1], z_out.shape[3], z_out.shape[4])
+            o_out[0] = o[...]
+
+
+def late(wz, wo, deps):
+    bits, z_blocks = wz
+    o_blocks = wo[1]
+    places = jnp.stack([jnp.stack(pair) for pair in bits]).astype(jnp.int32)
+    z_rows, z_cols = z_blocks[0].shape
+    o_rows, o_cols = o_blocks[0].shape
+
+    def kernel(places, *refs):
+        late_kernel(places, *refs[:8], *refs[8 + len(deps) :])
+
+    return pl.pallas_call(
+        kernel,
+        grid_spec=pltpu.PrefetchScalarGridSpec(
+            num_scalar_prefetch=1,
+            grid=(4,),
+            in_specs=[pl.BlockSpec((z_rows, z_cols), lambda i, at: (0, 0))] * 4
+            + [pl.BlockSpec((o_rows, o_cols), lambda i, at: (0, 0))] * 4
+            + [pl.BlockSpec(memory_space=pl.ANY)] * len(deps),
+            out_specs=[
+                pl.BlockSpec(
+                    (1, 2, 1, z_rows // 2, z_cols), lambda i, at: (at[i, 0], 0, at[i, 1], 0, 0)
+                ),
+                pl.BlockSpec((1, o_rows, o_cols), lambda i, at: (at[i, 0] * 2 + at[i, 1], 0, 0)),
+            ],
+        ),
+        out_shape=[
+            jax.ShapeDtypeStruct((2, 2, 2, z_rows // 2, z_cols), bf16),
+            jax.ShapeDtypeStruct((4, o_rows, o_cols), bf16),
+        ],
+        compiler_params=pltpu.CompilerParams(
+            dimension_semantics=("arbitrary",), vmem_limit_bytes=VMEM_LIMIT
+        ),
+        cost_estimate=cost(4),
+    )(places, *z_blocks, *o_blocks, *deps)
+
+
+def packed_rows(rows, out):
+    across = rows.shape[1] // 128
+    blocks, height = out.shape[1], out.shape[2]
+    tile = 0
+    for block in range(blocks):
+        for row in range(0, height, 16):
+            for lane in range(0, SMALL, 128):
+                r, c = tile // across * 16, tile % across * 128
+                out[0, block, row : row + 16, lane : lane + 128] = rows[r : r + 16, c : c + 128]
+                tile += 1
+
+
+def pack_rows(small):
+    blocks, height, _ = small.shape
+    tiles = small.reshape(blocks, height // 16, 16, SMALL // 128, 128)
+    tiles = jnp.moveaxis(tiles, 3, 2).reshape(-1, D // 128, 16, 128)
+    return jnp.moveaxis(tiles, 1, 2).reshape(-1, D)
+
+
+def spread_sum(value, axes):
+    parts = lax.all_to_all(value.astype(bf16), axes, split_axis=0, concat_axis=0, tiled=True)
+    return jnp.sum(parts.astype(f32), axis=0)
+
+
+def over_y(value):
+    y, other = flip("y")
+    value = value.astype(bf16)
+    got = swapped(lax.dynamic_index_in_dim(value, other, 1, False), "y")
+    return lax.dynamic_index_in_dim(value, y, 1, False).astype(f32) + got.astype(f32)
+
+
+def over_z(value):
+    zh, other = flip("zh")
+    got = swapped(lax.dynamic_index_in_dim(value, other, 0, False).astype(bf16), "zh")
+    return lax.dynamic_index_in_dim(value, zh, 0, False) + got.astype(f32)
+
+
+def row_sum(value):
+    if is_square(ROW):
+        return over_z(over_y(value))
+    return spread_sum(value.reshape((-1,) + value.shape[2:]), ROW)
+
+
+def stacked(gathered):
+    bits, blocks = gathered
+    result = jnp.zeros((len(blocks),) + blocks[0].shape, blocks[0].dtype)
+    for (zh, y), block in zip(bits, blocks):
+        result = lax.dynamic_update_index_in_dim(result, block, zh * 2 + y, 0)
+    return result
+
+
+def after(value, *others, us=0):
+    others = [other for other in others if other is not None]
+    if not others and not us:
+        return value
+    anywhere = pl.BlockSpec(memory_space=pl.ANY)
+    return pl.pallas_call(
+        lambda *refs: None,
+        in_specs=[anywhere] * (1 + len(others)),
+        out_specs=anywhere,
+        out_shape=jax.ShapeDtypeStruct(value.shape, value.dtype),
+        input_output_aliases={0: 0},
+        cost_estimate=cost(us),
+    )(value, *others)
+
+
+def carried_over(memory, packed):
+    packed = packed.astype(f32)
+    fall = jnp.sum(packed[:, STATE : STATE + 3], axis=1, keepdims=True)
+    return fall * memory + packed[:, :STATE]
+
+
 def three_parts(value):
     high = lax.reduce_precision(value, 8, 7)
     middle = lax.reduce_precision(value - high, 8, 7)
@@ -453,6 +828,35 @@
     return jnp.stack([high, middle, low]).astype(bf16)
 
 
+def multiply(a, rights, on_a, block, deps=(), us=0):
+    size = a.shape[1 - on_a]
+    count = len(rights)
+
+    def kernel(*refs):
+        left = refs[0][...]
+        outs = refs[1 + count + len(deps) :]
+        for right, out in zip(refs[1 : 1 + count], outs):
+            out[...] = dot(left, right[...], on_a, 0).astype(bf16)
+
+    if on_a:
+        left_spec = pl.BlockSpec((block, a.shape[1]), lambda i: (i, 0))
+    else:
+        left_spec = pl.BlockSpec((a.shape[0], block), lambda i: (0, i))
+    return pl.pallas_call(
+        kernel,
+        grid=(size // block,),
+        in_specs=[left_spec]
+        + [pl.BlockSpec(right.shape, lambda i: (0, 0)) for right in rights]
+        + [pl.BlockSpec(memory_space=pl.ANY)] * len(deps),
+        out_specs=[pl.BlockSpec((block, right.shape[1]), lambda i: (i, 0)) for right in rights],
+        out_shape=[jax.ShapeDtypeStruct((size, right.shape[1]), bf16) for right in rights],
+        compiler_params=pltpu.CompilerParams(
+            dimension_semantics=("arbitrary",), vmem_limit_bytes=VMEM_LIMIT
+        ),
+        cost_estimate=cost(us),
+    )(a, *rights, *deps)
+
+
 def product(a, b, on_a, on_b):
     return lax.dot_general(a, b, (((on_a,), (on_b,)), ((), ())), preferred_element_type=f32)
 
@@ -461,41 +865,57 @@
     x_in, lengths, cotangent, w_in, m_in, v_in, w_out, m_out, v_out, conv_w, m_conv, v_conv,
     vectors, m_vec, v_vec, head_params, m_head, v_head,
 ):
-    zn = lax.axis_size("z")
-    head_size = lax.axis_size("head")
-    qn = lax.axis_size("y") * head_size
-    devices = zn * qn
+    row_shape = (lax.axis_size("zh"), lax.axis_size("y"))
+    row_count = row_shape[0] * row_shape[1]
+    head_size = lax.axis_size("x") * lax.axis_size("core")
+    q_shape = (lax.axis_size("zl"), head_size)
+    qn = q_shape[0] * head_size
+    devices = row_count * qn
     q = lax.axis_index(Q)
-    z = lax.axis_index("z")
     groups, own, _ = x_in.shape
-    span = own * qn
     sequences = lengths.shape[1]
+    span = own * head_size
+    runs = q_shape[0] * groups
     chunks = span // CHUNK
     part = CHUNK // own
-    tokens = groups * span
+    tokens = groups * own * qn
     width = INNER // qn
     heads_own = HEADS // qn
     unit = INNER // devices
+    square = is_square(ROW + Q)
     strided = unit % HEAD_DIM == 0
     rows_in = D // devices
     conv_rows, vec_rows, head_cols = conv_w.shape[0], vectors.shape[0], head_params.shape[1]
+    full_shape = (row_shape[0], q_shape[0], row_shape[1], head_size)
 
     def split(array, size):
         lead = array.shape[:-1]
+        n = len(lead)
         if strided:
-            array = array.reshape(lead + (zn, qn, size // devices))
+            array = array.reshape(lead + full_shape + (size // devices,))
+            order = (n + 1, n + 3) + tuple(range(n)) + (n, n + 2, n + 4)
+            array = array.transpose(order)
         else:
-            array = array.reshape(lead + (1, qn, size // qn))
-        return jnp.moveaxis(array, -2, 0).reshape((qn,) + lead + (size // qn,))
+            array = jnp.moveaxis(array.reshape(lead + (qn, size // qn)), -2, 0)
+        return array.reshape((qn,) + lead + (size // qn,))
 
     def join(array, size):
         lead = array.shape[1:-1]
-        count = zn if strided else 1
-        array = array.reshape((qn,) + lead + (count, size // (qn * count)))
-        return jnp.moveaxis(array, 0, -2).reshape(lead + (size,))
+        n = len(lead)
+        if strided:
+            array = array.reshape(q_shape + lead + row_shape + (size // devices,))
+            order = tuple(range(2, 2 + n)) + (2 + n, 0, 3 + n, 1, 4 + n)
+            array = array.transpose(order)
+        else:
+            array = jnp.moveaxis(array, 0, -2)
+        return array.reshape(lead + (size,))
 
     def own_of(array, size):
         return lax.dynamic_index_in_dim(split(array, size), q, 0, False)
+
+    def by_rows(array):
+        array = array.reshape(row_shape + q_shape + array.shape[2:])
+        return jnp.swapaxes(array, 1, 2)
 
     own_heads = own_of(jnp.arange(HEADS, dtype=jnp.int32), HEADS)
 
@@ -508,9 +928,29 @@
     )
     payload = jnp.pad(payload, (0, rows_in * HEADS - payload.shape[0])).reshape(rows_in, HEADS)
     small_own = jnp.concatenate([w_in[:, 2 * INNER :].astype(bf16), payload], axis=1)
-    small_all = lax.all_gather(small_own, ALL, axis=0, tiled=False)
-    w_small = small_all.reshape(D, SMALL)
-    payload = small_all[:, :, SMALL - HEADS :].reshape(devices, rows_in * HEADS)
+    if square:
+        small_row = stacked(gather_row(small_own)[0])
+    else:
+        small_row = lax.all_gather(small_own, ROW, axis=0, tiled=False)
+    payload_rows = small_row[:, :, SMALL - HEADS :].reshape(1, -1, width)
+    payload_rows = jnp.broadcast_to(payload_rows, (qn,) + payload_rows.shape[1:])
+    both = [split(w_in[:, first : first + INNER].astype(bf16), INNER) for first in (INNER, 0)]
+    both = jnp.concatenate(both + [payload_rows], axis=1)
+    both = lax.all_to_all(both, Q, split_axis=0, concat_axis=0, tiled=True)
+    payload = both[:, 2 * rows_in :].reshape(q_shape + row_shape + (rows_in * HEADS,))
+    payload = payload.transpose(2, 0, 3, 1, 4).reshape(devices, -1)
+    w_x_own, w_z_own = both[:, :rows_in], both[:, rows_in : 2 * rows_in]
+    w_out_b = w_out.astype(bf16)
+    if square:
+        w_x, hops_x = gather_row(w_x_own.reshape(-1, width))
+        w_z, hops_z = gather_row(after(w_z_own.reshape(-1, width), *hops_x))
+        w_o, hops_o = gather_row(after(w_out_b, *hops_z))
+    else:
+        hops_z, hops_o = (), ()
+        w_x, w_z = (lax.all_gather(w, ROW, axis=0, tiled=False) for w in (w_x_own, w_z_own))
+        w_x, w_z = (by_rows(w).reshape(D, width) for w in (w_x, w_z))
+        w_o = lax.all_gather(w_out_b, ALL, axis=0, tiled=True)
+        w_o = lax.dynamic_slice_in_dim(w_o, q * width, width, 0)
     cut = [conv_rows * KW, vec_rows, 9 * head_cols]
     taps = jnp.moveaxis(payload[:, : cut[0]].reshape(devices, KW, conv_rows), 0, 1)
     taps = taps.reshape(KW, CONV).astype(f32)
@@ -531,45 +971,60 @@
         jnp.where(jnp.arange(HEADS)[:, None] == head_of_lane[None, :], params[:, :, None], 0.0), 1
     )
     hp = jnp.pad(hp, ((0, 5), (0, 0)))
-    spread = (lanes[:, None] == jnp.arange(width)[None, :] // HEAD_DIM).astype(f32)
-    offsets = (jnp.cumsum(lengths, axis=1) - lengths - z * span).astype(jnp.int32)
-
-    x_all = lax.all_gather(x_in, Q, axis=0, tiled=False).reshape(tokens, D)
-    cot_all = lax.all_gather(cotangent, Q, axis=0, tiled=False).reshape(tokens, D)
-
-    def columns(first):
-        mine = split(w_in[:, first : first + INNER].astype(bf16), INNER)
-        mine = lax.all_to_all(mine, Q, split_axis=0, concat_axis=0, tiled=True)
-        return lax.all_gather(mine, "z", axis=0, tiled=False).reshape(D, width)
-
-    w_x = columns(INNER)
-    w_z = columns(0)
-    if strided:
-        w_o = lax.all_gather(w_out.astype(bf16), "z", axis=0, tiled=True)
+    spread = (lanes[:, None] == jnp.arange(width)[None, :] // HEAD_DIM).astype(bf16)
+    spread = jnp.concatenate([spread, spread], axis=0)
+    starts = jnp.arange(q_shape[0]) + lax.axis_index("zh") * q_shape[0]
+    starts = (starts * row_shape[1] + lax.axis_index("y")) * span
+    offsets = jnp.cumsum(lengths, axis=1) - lengths
+    offsets = offsets[None] - starts[:, None, None]
+    offsets = offsets.reshape(runs, sequences).astype(jnp.int32)
+
+    x_flat = x_in.reshape(groups * own, D)
+    if square:
+        joined = after(jnp.concatenate([x_flat, pack_rows(small_row)], axis=0), both)
+        x_all, normed, w_small, w_x = front(
+            gather_q(joined, hops_x + (norm_gain,), w_x[1][3:]), w_x, norm_gain, groups * own, row_count
+        )
+        w_x = w_x.reshape(D, width)
+        x_all, normed = x_all.reshape(tokens, D), normed.reshape(tokens, D)
+        w_small = jnp.swapaxes(w_small, 0, 1)
     else:
-        w_o = lax.all_gather(w_out.astype(bf16), ALL, axis=0, tiled=True)
-        w_o = lax.dynamic_slice_in_dim(w_o, q * width, width, 0)
-
-    x_float = x_all.astype(f32)
-    x_scaled = x_float * lax.rsqrt(jnp.mean(x_float * x_float, axis=-1, keepdims=True) + EPS)
-    normed = (x_scaled * norm_gain).astype(bf16)
+        x_all = lax.all_gather(x_flat, Q, axis=0, tiled=True)
+        w_small = lax.all_gather(small_own, ROW + Q, axis=0, tiled=False)
+        w_small = w_small.reshape(row_count, qn, rows_in, SMALL)
+    w_small = by_rows(w_small).reshape(D, SMALL)
+    if not square:
+        x_float = x_all.astype(f32)
+        scale = lax.rsqrt(jnp.mean(x_float * x_float, axis=-1, keepdims=True) + EPS)
+        normed = (x_float * scale * norm_gain).astype(bf16)
     token_shape = (qn, groups, own)
-    x_raw = product(normed, w_x, 1, 0).astype(bf16).reshape(token_shape + (width,))
-    s_raw = product(normed, w_small, 1, 0).astype(bf16).reshape(token_shape + (SMALL,))
-    x_halo = shifted_along(x_raw[qn - 1, :, own - EDGE :], "z", 1)
-    s_halo = shifted_along(s_raw[qn - 1, :, own - EDGE :], "z", 1)
+    x_raw, s_raw = multiply(normed, (w_x, w_small), 1, 256)
+    x_raw = x_raw.reshape(token_shape + (width,))
+    s_raw = s_raw.reshape(token_shape + (SMALL,))
+
+    def last_rows(raw):
+        raw = raw.reshape(q_shape + raw.shape[1:])
+        return raw[:, head_size - 1, :, own - EDGE :]
+
+    halo = halo_before(jnp.concatenate([last_rows(x_raw), last_rows(s_raw)], axis=-1))
+    halo = halo.reshape(runs, EDGE, width + SMALL)
+    x_halo, s_halo = halo[..., :width], halo[..., width:]
 
     def at(reverse):
         return (lambda i: chunks - 1 - i) if reverse else (lambda i: i)
 
     def token_spec(cols, reverse):
-        return pl.BlockSpec((part, 1, own, cols), lambda g, i: (at(reverse)(i), g, 0, 0))
+        def place(g, i):
+            return (lax.div(g, groups) * chunks + at(reverse)(i), lax.rem(g, groups), 0, 0)
+
+        return pl.BlockSpec((part, 1, own, cols), place)
 
     def before_spec(cols, reverse):
-        return pl.BlockSpec(
-            (1, 1, EDGE, cols),
-            lambda g, i: (jnp.maximum(part * at(reverse)(i) - 1, 0), g, own // EDGE - 1, 0),
-        )
+        def place(g, i):
+            block = lax.div(g, groups) * head_size + part * at(reverse)(i) - 1
+            return (jnp.maximum(block, 0), lax.rem(g, groups), own // EDGE - 1, 0)
+
+        return pl.BlockSpec((1, 1, EDGE, cols), place)
 
     def group_spec(*dims):
         return pl.BlockSpec((1,) + dims, lambda g, i: (g,) + (0,) * len(dims))
@@ -588,58 +1043,64 @@
     def s_specs(reverse):
         return [token_spec(SMALL, reverse), before_spec(SMALL, reverse), group_spec(EDGE, SMALL)]
 
-    head_specs = [whole_spec(8, 128), whole_spec(128, 128), whole_spec(128, width)]
+    head_specs = [whole_spec(8, 128), whole_spec(128, 128), whole_spec(256, width)]
     x_args = (x_raw, x_raw, x_halo)
     s_args = (s_raw, s_raw, s_halo)
     head_args = (hp, pick, spread)
     state_ref = pltpu.VMEM((STATE, width), f32)
     fall_ref = pltpu.VMEM((8, width), f32)
 
-    def call(kernel, in_specs, out_specs, out_shape, scratch, flops, moved):
-        return pl.pallas_call(
-            functools.partial(kernel, sequences),
-            grid=(groups, chunks),
-            in_specs=in_specs,
+    def call(kernel, us, in_specs, out_specs, out_shape, scratch, deps=()):
+        count = len(in_specs)
+        anywhere = [pl.BlockSpec(memory_space=pl.ANY)] * len(deps)
+
+        def body(*refs):
+            kernel(sequences, *refs[:count], *refs[count + len(deps) :])
+
+        call = pl.pallas_call(
+            body,
+            grid=(runs, chunks),
+            in_specs=in_specs + anywhere,
             out_specs=out_specs,
             out_shape=out_shape,
             scratch_shapes=scratch,
             compiler_params=pltpu.CompilerParams(
                 dimension_semantics=("arbitrary", "arbitrary"), vmem_limit_bytes=VMEM_LIMIT
             ),
-            cost_estimate=pl.CostEstimate(flops=flops, bytes_accessed=moved, transcendentals=0),
+            cost_estimate=cost(us),
         )
+        return lambda *args: call(*args, *deps)
 
     with jax.named_scope("memory_own"):
         ended = call(
-            state_kernel,
+            state_kernel, 0,
             [offs_spec] + x_specs(False) + s_specs(False)
             + [whole_spec(8, width), whole_spec(8, MIX)] + head_specs,
             group_spec(STATE + EDGE, width),
-            jax.ShapeDtypeStruct((groups, STATE + EDGE, width), bf16),
+            jax.ShapeDtypeStruct((runs, STATE + EDGE, width), bf16),
             [state_ref, fall_ref],
-            4_000_000_000, 4_000_000,
         )(offsets, *x_args, *s_args, taps_x, taps_s, *head_args)
-    ended_all = lax.all_gather(ended, "z", axis=0, tiled=False).astype(f32)
-    falls = jnp.sum(ended_all[:, :, STATE : STATE + 3], axis=2, keepdims=True)
-    incoming = jnp.zeros((groups, STATE, width), f32)
-    for k in range(zn - 1):
-        joined = falls[k] * incoming + ended_all[k, :, :STATE]
-        incoming = jnp.where(k < z, joined, incoming)
+    cot_flat = after(cotangent.reshape(groups * own, D), x_all)
+    cot_all = lax.all_gather(cot_flat, Q, axis=0, tiled=False).reshape(tokens, D)
+    ended = ended.reshape(q_shape[0], groups, STATE + EDGE, width)
+    incoming, _, _ = passed(ended, False, hops_z)
 
     with jax.named_scope("scan"):
         scanned, kept = call(
-            scan_kernel,
+            scan_kernel, 0,
             [offs_spec] + x_specs(False) + s_specs(False)
             + [whole_spec(8, width), whole_spec(8, MIX)] + head_specs + [group_spec(STATE, width)],
             [token_spec(width, False), kept_spec(False)],
             [
                 jax.ShapeDtypeStruct(token_shape + (width,), bf16),
-                jax.ShapeDtypeStruct((groups, chunks, STATE, width), f32),
+                jax.ShapeDtypeStruct((runs, chunks, STATE, width), f32),
             ],
             [state_ref],
-            8_000_000_000, 6_000_000,
         )(offsets, *x_args, *s_args, taps_x, taps_s, *head_args, incoming)
 
+    if square:
+        w_z, w_o = late(w_z, w_o, (scanned,))
+        w_z, w_o = w_z.reshape(D, width), w_o.reshape(width, D)
     gate_in = product(normed, w_z, 1, 0)
     grad_gnorm = product(cot_all, w_o, 1, 1)
     scan_b = scanned.reshape(tokens, width).astype(f32)
@@ -658,91 +1119,101 @@
     slope = gate_sig * (1.0 + gate_in * (1.0 - gate_sig))
     grad_z = (grad_gated * scan_b * slope).astype(bf16)
 
-    branch = product(gnorm, w_o, 1, 0).astype(bf16).reshape(qn, groups, own, D)
+    with jax.named_scope("memory_back"):
+        direct = call(
+            direct_kernel, 8,
+            [offs_spec] + s_specs(False) + [whole_spec(8, MIX)] + head_specs
+            + [token_spec(width, False)],
+            group_spec(STATE + EDGE, width),
+            jax.ShapeDtypeStruct((runs, STATE + EDGE, width), bf16),
+            [state_ref, fall_ref],
+        )(offsets, *s_args, taps_s, *head_args, grad_scan)
+    grad_out = multiply(gnorm, (cot_all,), 0, 128, (direct,))[0]
+    branch = multiply(gnorm, (w_o,), 1, 256, (direct,))[0].reshape(qn, groups, own, D)
+    own_z = multiply(normed, (grad_z,), 0, 256, (direct,))[0]
+    def sum_out(met):
+        value = after(grad_out, met)
+        if square:
+            return over_y(value.reshape(row_shape + (unit, D)))
+        if strided:
+            return row_sum(value.reshape(row_shape + (unit, D)))
+        full = jnp.zeros((INNER, D), bf16)
+        full = lax.dynamic_update_slice_in_dim(full, value, q * width, 0)
+        return spread_sum(full.reshape(devices, unit, D), ALL)
+
+    later, met, half_out = passed(
+        direct.reshape(q_shape[0], groups, STATE + EDGE, width),
+        True,
+        (grad_out, own_z),
+        (branch,),
+        sum_out,
+    )
+    own_z = after(own_z, met)
+    branch = after(branch, later)
     branch = lax.psum_scatter(branch, Q, scatter_dimension=0, tiled=False)
     result = (x_in.astype(f32) + branch.astype(f32)).astype(bf16)
-    grad_out = product(gnorm, cot_all, 0, 0).astype(bf16)
-    if strided:
-        grad_out = lax.psum_scatter(grad_out, "z", scatter_dimension=0, tiled=True)
-    else:
-        full = jnp.zeros((INNER, D), bf16)
-        full = lax.dynamic_update_slice_in_dim(full, grad_out, q * width, 0)
-        grad_out = lax.psum_scatter(full, ALL, scatter_dimension=0, tiled=True)
-
-    with jax.named_scope("memory_back"):
-        direct = call(
-            direct_kernel,
-            [offs_spec] + s_specs(False) + [whole_spec(8, MIX)] + head_specs
-            + [token_spec(width, False)],
-            group_spec(STATE, width),
-            jax.ShapeDtypeStruct((groups, STATE, width), bf16),
-            [state_ref, fall_ref],
-            2_000_000_000, 3_000_000,
-        )(offsets, *s_args, taps_s, *head_args, grad_scan)
-    direct_all = lax.all_gather(direct, "z", axis=0, tiled=False).astype(f32)
-    later = jnp.zeros((groups, STATE, width), f32)
-    for k in range(zn - 1, 0, -1):
-        joined = falls[k] * later + direct_all[k]
-        later = jnp.where(k > z, joined, later)
+    grad_out = over_z(half_out) if square else half_out
+
+    def line_blocks(grad):
+        cols = grad.shape[1]
+        grad = grad.reshape(row_shape[0], q_shape[0], row_shape[1], head_size * rows_in, cols)
+        if square:
+            return over_y(jnp.swapaxes(grad, 1, 2))
+        return row_sum(jnp.swapaxes(grad, 1, 2)).reshape(qn, rows_in, cols)
+
+    def line_rest(early, *deps):
+        early = after(early, *deps)
+        return (over_z(early) if square else early).reshape(qn, rows_in, early.shape[-1])
 
     def home(grad):
-        cols = grad.shape[1]
-        grad = grad.astype(bf16).reshape(zn, qn, rows_in, cols)
-        grad = lax.psum_scatter(grad, "z", scatter_dimension=0, tiled=False)
-        return lax.all_to_all(grad, Q, split_axis=0, concat_axis=0, tiled=True)
-
-    home_z = home(product(normed, grad_z, 0, 0))
+        return lax.all_to_all(grad.astype(bf16), Q, split_axis=0, concat_axis=0, tiled=True)
+
+    early_z = line_blocks(own_z)
+    home_z = home(line_rest(early_z))
 
     with jax.named_scope("scan_back"):
-        dx, ds, tail_x, tail_s, rim_x, rim_s, gx, gs, gh = call(
-            back_kernel,
+        dx, tail, rim, gx, gs, gh = call(
+            back_kernel, 22,
             [offs_spec] + x_specs(True) + s_specs(True)
             + [whole_spec(8, width), whole_spec(8, MIX)] + head_specs
             + [token_spec(width, True), kept_spec(True), group_spec(STATE, width)],
             [
-                token_spec(width, True), token_spec(SMALL, True),
-                group_spec(EDGE, width), group_spec(EDGE, MIX),
-                group_spec(EDGE, width), group_spec(EDGE, MIX),
+                token_spec(width + SMALL, True),
+                group_spec(EDGE, width + MIX), group_spec(EDGE, width + MIX),
                 whole_spec(8, width), whole_spec(8, MIX), whole_spec(8, 128),
             ],
             [
-                jax.ShapeDtypeStruct(token_shape + (width,), bf16),
-                jax.ShapeDtypeStruct(token_shape + (SMALL,), bf16),
-                jax.ShapeDtypeStruct((groups, EDGE, width), f32),
-                jax.ShapeDtypeStruct((groups, EDGE, MIX), f32),
-                jax.ShapeDtypeStruct((groups, EDGE, width), f32),
-                jax.ShapeDtypeStruct((groups, EDGE, MIX), f32),
+                jax.ShapeDtypeStruct(token_shape + (width + SMALL,), bf16),
+                jax.ShapeDtypeStruct((runs, EDGE, width + MIX), f32),
+                jax.ShapeDtypeStruct((runs, EDGE, width + MIX), f32),
                 jax.ShapeDtypeStruct((8, width), f32),
                 jax.ShapeDtypeStruct((8, MIX), f32),
                 jax.ShapeDtypeStruct((8, 128), f32),
             ],
             [state_ref, pltpu.VMEM((8, width), f32), pltpu.VMEM((8, MIX), f32)],
-            16_000_000_000, 9_000_000,
+            (half_out,),
         )(offsets, *x_args, *s_args, taps_x, taps_s, *head_args, grad_scan, kept, later)
-    rim_x, rim_s = shifted_along(rim_x, "z", -1), shifted_along(rim_s, "z", -1)
-    dx = dx.at[qn - 1, :, own - EDGE :].set((tail_x + rim_x).astype(bf16))
-    ds = ds.at[qn - 1, :, own - EDGE :, :MIX].set((tail_s + rim_s).astype(bf16))
-    grad_x = dx.reshape(tokens, width)
-    grad_s = ds.reshape(tokens, SMALL)
-
-    home_x = home(product(normed, grad_x, 0, 0))
-    home_s = home(product(normed, grad_s, 0, 0))
-    grad_in = jnp.concatenate(
-        [
-            join(home_z, INNER),
-            join(home_x, INNER),
-            jnp.sum(home_s.astype(f32), axis=0)[:, : MIX + HEADS].astype(bf16),
-        ],
-        axis=1,
+    tail = tail.reshape(q_shape[0], groups, EDGE, width + MIX)
+    rim = halo_after(after(rim, early_z, grad_out).reshape(q_shape[0], groups, EDGE, width + MIX))
+    tail = (tail + rim).astype(bf16)
+    for zl in range(q_shape[0]):
+        last = (zl + 1) * head_size - 1
+        dx = dx.at[last, :, own - EDGE :, : width + MIX].set(tail[zl])
+    grad_x = dx.reshape(tokens, width + SMALL)
+
+    own_x = multiply(normed, (grad_x,), 0, 256)[0]
+    early_x = line_blocks(own_x[:, :width])
+    own_s = own_x[:, width:].reshape(full_shape + (rows_in, SMALL)).transpose(1, 3, 0, 2, 4, 5)
+    own_s = spread_sum(own_s.reshape(qn, row_count, rows_in, SMALL), Q)
+    home_s = row_sum(own_s.reshape(row_shape + (rows_in, SMALL)))
+    grad_normed, gain_sums = back_projection(
+        (grad_z, grad_x), (w_z, w_x, w_small), x_all, (branch, own_x)
+    )
+    grad_own = lax.psum_scatter(
+        grad_normed.reshape(qn, groups, own, D), Q, scatter_dimension=0, tiled=False
     ).astype(f32)
 
-    grad_normed = (
-        product(grad_z, w_z, 1, 1) + product(grad_x, w_x, 1, 1) + product(grad_s, w_small, 1, 1)
-    )
-    grad_norm_gain = jnp.sum(grad_normed * x_scaled, axis=0)
-    grad_own = lax.psum_scatter(
-        grad_normed.astype(bf16).reshape(qn, groups, own, D), Q, scatter_dimension=0, tiled=False
-    ).astype(f32)
+    grad_norm_gain = jnp.sum(gain_sums, axis=0)
     x_own = x_in.astype(f32)
     inverse = lax.rsqrt(jnp.mean(x_own * x_own, axis=-1, keepdims=True) + EPS)
     grad_unit = grad_own * norm_gain
@@ -771,12 +1242,20 @@
     )
     used = packed.shape[1]
     packed = jnp.pad(packed, ((0, 0), (0, -used % 1024))).reshape(devices, -1, 128)
-    packed = lax.psum_scatter(packed, ALL, scatter_dimension=0, tiled=False).reshape(-1)
+    packed = lax.all_to_all(packed, ALL, split_axis=0, concat_axis=0, tiled=True)
+    packed = jnp.sum(packed, axis=0).reshape(-1)
     grad_conv = packed[: conv_rows * KW].reshape(KW, conv_rows).T
     grad_vec = packed[conv_rows * KW : conv_rows * KW + vec_rows]
     grad_head = packed[conv_rows * KW + vec_rows : used].reshape(3, head_cols)
 
-    in_new = adam(w_in, m_in, v_in, grad_in, rate_input)
+    home_x = home(line_rest(early_x, grad_normed))
+    if square:
+        in_new = adam_columns((w_in, m_in, v_in), home_z, None, 0, None)
+        in_new = adam_columns((w_in, m_in, v_in), home_x, home_s, 4, in_new)
+    else:
+        grad_in = [join(home_z, INNER).astype(f32), join(home_x, INNER).astype(f32)]
+        grad_in = jnp.concatenate(grad_in + [home_s[:, : MIX + HEADS]], axis=1)
+        in_new = adam(w_in, m_in, v_in, grad_in, rate_input)
     out_new = adam(w_out, m_out, v_out, grad_out.astype(f32), rate_output)
     conv_new = adam(conv_w, m_conv, v_conv, grad_conv, rate_conv)
     vec_new = adam(vectors, m_vec, v_vec, grad_vec, rate_vector)
@@ -786,9 +1265,9 @@
 
 def solution(mesh):
     seq, head = mesh.shape["seq"], mesh.shape["head"]
-    fine = Mesh(mesh.devices.reshape(seq // 2, 2, head), ALL)
+    fine = Mesh(mesh.devices.reshape(2, 2, seq // 4, head // 2, 2), ALL)
     token, row = P(None, ALL, None), P(ALL, None)
-    line, heads = P(ALL), P(None, "head")
+    line, heads = P(ALL), P(None, ("x", "core"))
     return jax.shard_map(
         local,
         mesh=fine,

time: 856 us -> 521 us (0.61)
  waiting for transfers between devices: 570 us -> 163 us
  matrix products: 73.6 us -> 9.63 us
  starting transfers between devices: 20.6 us -> 78.3 us
  Pallas kernels: 69.2 us -> 117 us
  local copies, waits for them, and re-layouts: 17 us -> 58 us
  blocking collectives: 42.6 us -> 12.9 us
  other arithmetic: 38.7 us -> 57.1 us
    all_gather x8 -> x1, waiting for transfers between devices: 228 us -> 0.01 us  [local(): lax.all_gather(cot_flat, Q, axis=0, tiled=False).reshape(tokens, D)]
    reduce_scatter x5 -> x1, waiting for transfers between devices: 166 us -> 0.01 us  [local(): lax.psum_scatter(grad_normed.reshape(qn, groups, own, D), Q, scatter_dime...]
    ppermute x4 -> x35, waiting for transfers between devices: 4.6 us -> 146 us  [the longest x27 139 us: swapped(): return lax.ppermute(value, axis, [(0, 1), (1, 0)])]
    unnamed x16 -> x3, waiting for transfers between devices: 118 us -> 0.05 us
    dot_general x12 -> x2, matrix products: 73.6 us -> 9.63 us  [product(): lax.dot_general(a, b, (((on_a,), (on_b,)), ((), ())), preferred_element_t...]
    reduce_scatter x1, waiting for transfers between devices: 53.1 us -> 0.01 us  [local(): branch = lax.psum_scatter(branch, Q, scatter_dimension=0, tiled=False)]
    pallas_call x4 -> x28, Pallas kernels: 69.2 us -> 117 us  [the longest x4 52.1 us: call(): return lambda *args: call(*args, *deps)]
    ppermute x4 -> x35, starting transfers between devices: 7.74 us -> 52.2 us  [the longest x27 40.6 us: swapped(): return lax.ppermute(value, axis, [(0, 1), (1, 0)])]
  transfers between devices with their start and end apart: 22 -> 43, of which waited for: 16 -> 18; matrix products, arithmetic and copies ran while one was open for 12% -> 14% of each run, Pallas kernels for 3% -> 17%
where the time goes in v2:
time: 521 us; the launch traced here: 511 us
  waiting for transfers between devices  163 us (31%)
  Pallas kernels  117 us (22%)
  starting transfers between devices  78.3 us (15%)
  local copies, waits for them, and re-layouts  58 us (11%)
  other arithmetic  57.1 us (11%)
  between operations  15.8 us (3%)
  blocking collectives  12.9 us (2%)
  matrix products  9.63 us (2%)
    ppermute x27, waiting for transfers between devices, swapped(): return lax.ppermute(value, axis, [(0, 1), (1, 0)])  139 us
    pallas_call x4, Pallas kernels, call(): return lambda *args: call(*args, *deps)  52.1 us
    ppermute x27, starting transfers between devices, swapped(): return lax.ppermute(value, axis, [(0, 1), (1, 0)])  40.6 us
    pallas_call x5, Pallas kernels, multiply(): pl.pallas_call(kernel, grid=(size // block,), in_specs=[left_spec] + [pl....  30.8 us
    unnamed x197, local copies, waits for them, and re-layouts  25.2 us
    all_to_all x1, waiting for transfers between devices, local(): both = lax.all_to_all(both, Q, split_axis=0, concat_axis=0, tiled=True)  16.1 us
    psum x1, blocking collectives, local(): sums = lax.psum(sums, Q) / INNER  12.9 us
    all_to_all x2, starting transfers between devices, home(): lax.all_to_all(grad.astype(bf16), Q, split_axis=0, concat_axis=0, tiled=T...  12.9 us
  transfers between devices with their start and end apart: 43, of which 18 were waited for; matrix products, arithmetic and copies ran while one was open for 14% of the time, Pallas kernels for 17%

profile of v2, /device:TPU:0, one launch (start us, length us, event | category | flops | bytes accessed | tf_op | source)
XLA Modules:
  0.0 511.3 jit_solution(10425912348422280458)
XLA Ops:
  30.2 16.1 %all-to-all-done.refs_1_ = bf16[8,160,512]{2,1,0:T(8,128)(2,1)S(1)} async-done(((bf16[8,160,512]{2,1,0:T(8,128)(2,1)}), bf16[8,160,512]{2,1,0:T(8,128)(2,1)S(1)}, u32[]{:S(2)}, u32[]{:S(2)}) %all-to-all-start) | async-done | bytes 1310752 | tf_op jit(solution)/shard_map/all_to_all | solution.py:939
  56.2 7.1 %collective-permute-done.7.refs_1_.refs_9_ = bf16[512,512]{1,0:T(8,128)(2,1)S(1)} collective-permute-done((bf16[512,512]{1,0:T(8,128)(2,1)S(1)}, bf16[512,512]{1,0:T(8,128)(2,1)S(1)}, u32[]{:S(2)}, u32[]{:S(2)}) %collective-permute-start.7) | collective-permute-done | bytes 524320 | tf_op jit(solution)/shard_map/ppermute | solution.py:623
  63.3 11.4 %collective-permute-done.8.refs_2_.refs_10_ = bf16[512,512]{1,0:T(8,128)(2,1)S(1)} collective-permute-done((bf16[512,512]{1,0:T(8,128)(2,1)S(1)}, bf16[512,512]{1,0:T(8,128)(2,1)S(1)}, u32[]{:S(2)}, u32[]{:S(2)}) %collective-permute-start.8) | collective-permute-done | bytes 524320 | tf_op jit(solution)/shard_map/ppermute | solution.py:623
  79.9 11.5 %collective-permute-done.11.refs_1_.refs_11_ = bf16[512,512]{1,0:T(8,128)(2,1)S(1)} collective-permute-done((bf16[512,512]{1,0:T(8,128)(2,1)}, bf16[512,512]{1,0:T(8,128)(2,1)S(1)}, u32[]{:S(2)}, u32[]{:S(2)}) %collective-permute-start.11) | collective-permute-done | bytes 524320 | tf_op jit(solution)/shard_map/ppermute | solution.py:623
  98.1 9.0 %shard_map.308 = (bf16[8,128,2048]{2,1,0:T(8,128)(2,1)}, bf16[8,128,2048]{2,1,0:T(8,128)(2,1)}, bf16[8,4,64,384]{3,2,1,0:T(8,128)(2,1)}, bf16[8,256,512]{2,1,0:T(8,128)(2,1)}) custom-call(s32[2,8]{1,0:T(2,128)S(1)} %pad_add_fusion.1.places, bf16[176,2048]{1,0:T(8,128)(2,1)S(1)} %copy-done.14, bf16[176,2048]{1,0:T(8,128)(2,1)} %collective-permute-done.3.refs_1_, ...), custom_call_target="tpu_custom_call" | custom-call | bytes 1000 | tf_op jit(solution)/shard_map/pallas_call | solution.py:688
  116.7 6.3 %shard_map.309 = (bf16[1024,512]{1,0:T(8,128)(2,1)S(1)}, bf16[1024,384]{1,0:T(8,128)(2,1)S(1)}) custom-call(bf16[1024,2048]{1,0:T(8,128)(2,1)} %bitcast.299, bf16[2048,512]{1,0:T(8,128)(2,1)S(1)} %bitcast.279, bf16[2048,384]{1,0:T(8,128)(2,1)S(1)} %bitcast.267), custom_call_target="tpu_custom_call" | custom-call | bytes 1000 | tf_op jit(solution)/shard_map/pallas_call | solution.py:845
  128.4 10.2 %memory_own.1 = bf16[4,144,512]{2,1,0:T(8,128)(2,1)} custom-call(s32[4,3]{1,0:T(4,128)S(1)} %copy-done.57, bf16[8,2,64,512]{3,2,1,0:T(8,128)(2,1)S(1)} %bitcast.261, bf16[8,2,64,512]{3,2,1,0:T(8,128)(2,1)S(1)} %bitcast.262, bf16[4,16,512]{2,1,0:T(8,128)(2,1)S(1)} %slice.375.refs_3_, bf16[8,2,64,384]{3,2,1,0:T(8,128)(2,1)S(1)} %bitcast.270, ...), custom_call_target="tpu_custom_call" | custom-call | bytes 1000 | tf_op jit(solution)/shard_map/memory_own/pallas_call | solution.py:1072
  149.9 16.5 %collective-permute-done.16.refs_1_ = bf16[512,512]{1,0:T(8,128)(2,1)} collective-permute-done((bf16[512,512]{1,0:T(8,128)(2,1)}, bf16[512,512]{1,0:T(8,128)(2,1)}, u32[]{:S(2)}, u32[]{:S(2)}) %collective-permute-start.16) | collective-permute-done | bytes 524320 | tf_op jit(solution)/shard_map/ppermute | solution.py:623
  184.2 9.3 %collective-permute-done.21.refs_6_ = bf16[128,2048]{1,0:T(8,128)(2,1)} collective-permute-done((bf16[128,2048]{1,0:T(8,128)(2,1)}, bf16[128,2048]{1,0:T(8,128)(2,1)}, u32[]{:S(2)}, u32[]{:S(2)}) %collective-permute-start.21) | collective-permute-done | bytes 524320 | tf_op jit(solution)/shard_map/ppermute | solution.py:623
  197.1 11.7 %scan.1 = (bf16[8,2,64,512]{3,2,1,0:T(8,128)(2,1)S(1)}, f32[4,2,128,512]{3,2,1,0:T(8,128)}) custom-call(s32[4,3]{1,0:T(4,128)S(1)} %copy-done.58, bf16[8,2,64,512]{3,2,1,0:T(8,128)(2,1)S(1)} %bitcast.263, bf16[8,2,64,512]{3,2,1,0:T(8,128)(2,1)S(1)} %bitcast.264, bf16[4,16,512]{2,1,0:T(8,128)(2,1)S(1)} %slice.375.refs_3_, ...), custom_call_target="tpu_custom_call" | custom-call | bytes 1000 | tf_op jit(solution)/shard_map/scan/pallas_call | solution.py:1072
  208.7 9.4 %collective-permute-done.22.refs_7_ = bf16[128,2048]{1,0:T(8,128)(2,1)S(1)} collective-permute-done((bf16[128,2048]{1,0:T(8,128)(2,1)}, bf16[128,2048]{1,0:T(8,128)(2,1)S(1)}, u32[]{:S(2)}, u32[]{:S(2)}) %collective-permute-start.22) | collective-permute-done | bytes 524320 | tf_op jit(solution)/shard_map/ppermute | solution.py:623
  223.6 5.4 %fusion.55 = f32[1024,512]{1,0:T(8,128)S(1)} fusion(bf16[1024,2048]{1,0:T(8,128)(2,1)} %all-gather.3.cloned.1.call-done.refs_1_, bf16[512,2048]{1,0:T(8,128)(2,1)} %bitcast.286), kind=kOutput, calls=%fused_computation.201 | convolution fusion | flops 2147483648 | bytes 8388608 | tf_op jit(solution)/shard_map/dot_general | solution.py:861
  233.9 12.9 %psum.7 = f32[2,1024]{1,0:T(2,128)} all-reduce(f32[2,1024]{1,0:T(2,128)} %pad_maximum_fusion.8), channel_id=1, replica_groups=mesh['zh'=2,'zl'=2,'y'=2,'x'=2,'core'=2] {'zl','x','core'}, use_global_device_ids=true, to_apply=%region_9.10 | all-reduce | flops 2048 | bytes 16384 | tf_op jit(solution)/shard_map/psum | solution.py:1112
  247.6 5.3 %fusion.1 = (bf16[1024,512]{1,0:T(8,128)(2,1)}, bf16[1024,512]{1,0:T(8,128)(2,1)S(1)}, f32[512]{0:T(512)}, bf16[1024,512]{1,0:T(8,128)(2,1)}) fusion(f32[1024,512]{1,0:T(8,128)} %get-tuple-element.137, bf16[8,2,64,512]{3,2,1,0:T(8,128)(2,1)} %copy-done.35, f32[1024]{0:T(1024)S(1)} %multiply_multiply_fusion.2, f32[1024,512]{1,0:T(8,128)} %copy-done.77, ...), kind=kLoop, calls=%fused_computation.3 | loop fusion | flops 12582400 | bytes 8400896 | tf_op jit(solution)/shard_map/convert_element_type | solution.py:1120
  252.9 8.1 %memory_back.1.refs_2_ = bf16[4,144,512]{2,1,0:T(8,128)(2,1)} custom-call(s32[4,3]{1,0:T(4,128)S(1)} %copy-done.59, bf16[8,2,64,384]{3,2,1,0:T(8,128)(2,1)S(1)} %bitcast.274, bf16[8,2,64,384]{3,2,1,0:T(8,128)(2,1)S(1)} %bitcast.275, bf16[4,16,384]{2,1,0:T(8,128)(2,1)S(1)} %slice.376.refs_6_.refs_3_, f32[8,256]{1,0:T(8,128)S(1)} %copy-done.47, ...), custom_call_target="tpu_custom_call" | custom-call | flops 3200000000 | bytes 1000 | tf_op jit(solution)/shard_map/memory_back/pallas_call | solution.py:1072
  263.0 6.8 %shard_map.317.refs_2_.refs_0_ = bf16[2048,512]{1,0:T(8,128)(2,1)S(1)} custom-call(bf16[1024,2048]{1,0:T(8,128)(2,1)} %bitcast.300, bf16[1024,512]{1,0:T(8,128)(2,1)S(1)} %copy-done.6, bf16[4,144,512]{2,1,0:T(8,128)(2,1)} %memory_back.1.refs_2_), custom_call_target="tpu_custom_call" | custom-call | bytes 1000 | tf_op jit(solution)/shard_map/pallas_call | solution.py:845
  275.2 5.4 %shard_map.316.refs_1_.refs_0_ = bf16[512,2048]{1,0:T(8,128)(2,1)S(1)} custom-call(bf16[1024,512]{1,0:T(8,128)(2,1)S(1)} %copy-done.8, bf16[1024,2048]{1,0:T(8,128)(2,1)} %all-gather.3.cloned.1.call-done.refs_1_, bf16[4,144,512]{2,1,0:T(8,128)(2,1)} %memory_back.1.refs_2_), custom_call_target="tpu_custom_call" | custom-call | bytes 1000 | tf_op jit(solution)/shard_map/pallas_call | solution.py:845
  288.6 19.3 %collective-permute-done.25 = bf16[2,128,2048]{2,1,0:T(8,128)(2,1)S(1)} collective-permute-done((bf16[2,128,2048]{2,1,0:T(8,128)(2,1)S(1)}, bf16[2,128,2048]{2,1,0:T(8,128)(2,1)S(1)}, u32[]{:S(2)}, u32[]{:S(2)}) %collective-permute-start.25) | collective-permute-done | bytes 1048608 | tf_op jit(solution)/shard_map/ppermute | solution.py:623
  318.8 22.2 %scan_back.1 = (bf16[8,2,64,896]{3,2,1,0:T(8,128)(2,1)}, f32[4,16,768]{2,1,0:T(8,128)S(1)}, f32[4,16,768]{2,1,0:T(8,128)S(1)}, f32[8,512]{1,0:T(8,128)S(1)}, f32[8,256]{1,0:T(8,128)S(1)}, /*index=5*/f32[8,128]{1,0:T(8,128)S(1)}) custom-call(s32[4,3]{1,0:T(4,128)S(1)} %copy-done.60, bf16[8,2,64,512]{3,2,1,0:T(8,128)(2,1)S(1)} %bitcast.265, ...), custom_call_target="tpu_custom_call" | custom-call | flops 8800000000 | bytes 1000 | tf_op jit(solution)/shard_map/scan_back/pallas_call | solution.py:1072
  354.0 8.2 %shard_map.324.refs_7_ = bf16[2048,896]{1,0:T(8,128)(2,1)S(1)} custom-call(bf16[1024,2048]{1,0:T(8,128)(2,1)} %bitcast.301, bf16[1024,896]{1,0:T(8,128)(2,1)S(1)} %bitcast.280), custom_call_target="tpu_custom_call" | custom-call | bytes 1000 | tf_op jit(solution)/shard_map/pallas_call | solution.py:845
  366.7 11.3 %shard_map.325 = (bf16[1024,2048]{1,0:T(8,128)(2,1)}, f32[8,2048]{1,0:T(8,128)S(1)}) custom-call(bf16[1024,512]{1,0:T(8,128)(2,1)S(1)} %copy-done.7, bf16[1024,896]{1,0:T(8,128)(2,1)S(1)} %bitcast.281, bf16[2048,512]{1,0:T(8,128)(2,1)} %bitcast.314, bf16[2048,512]{1,0:T(8,128)(2,1)} %bitcast.278, bf16[2048,384]{1,0:T(8,128)(2,1)S(1)} %bitcast.268, ...), custom_call_target="tpu_custom_call" | custom-call | bytes 1000 | tf_op jit(solution)/shard_map/pallas_call | solution.py:482
  398.8 24.8 %collective-permute-done.34 = bf16[2,256,512]{2,1,0:T(8,128)(2,1)S(1)} collective-permute-done((bf16[2,256,512]{2,1,0:T(8,128)(2,1)}, bf16[2,256,512]{2,1,0:T(8,128)(2,1)S(1)}, u32[]{:S(2)}, u32[]{:S(2)}) %collective-permute-start.34) | collective-permute-done | bytes 524320 | tf_op jit(solution)/shard_map/ppermute | solution.py:623
  424.6 9.4 %all-to-all-start.3 = ((bf16[8,64,512]{2,1,0:T(8,128)(2,1)}), bf16[8,64,512]{2,1,0:T(8,128)(2,1)S(1)}, u32[]{:S(2)}, u32[]{:S(2)}) async-start(bf16[8,64,512]{2,1,0:T(8,128)(2,1)} %bitcast.120), calls=%async_computation.5 | async-start | bytes 1048576 | tf_op jit(solution)/shard_map/all_to_all | solution.py:1169
  454.0 18.4 %collective-permute-done.31 = bf16[2,256,512]{2,1,0:T(8,128)(2,1)} collective-permute-done((bf16[2,256,512]{2,1,0:T(8,128)(2,1)}, bf16[2,256,512]{2,1,0:T(8,128)(2,1)}, u32[]{:S(2)}, u32[]{:S(2)}) %collective-permute-start.31) | collective-permute-done | bytes 524320 | tf_op jit(solution)/shard_map/ppermute | solution.py:623
  (488 shorter events, 219.8 us)
Async XLA Ops:
  29.0 194.6 %all-gather.3.cloned.1.call-start = ((), (), s32[]{:S(2)}) async-start(), calls=%async_computation.9 | async-start | bytes 4718592 | tf_op jit(solution)/shard_map/all_gather | solution.py:1084
  47.3 29.1 %collective-permute-start.6 = (bf16[176,2048]{1,0:T(8,128)(2,1)}, bf16[176,2048]{1,0:T(8,128)(2,1)S(1)}, u32[]{:S(2)}, u32[]{:S(2)}) collective-permute-start(bf16[176,2048]{1,0:T(8,128)(2,1)} %shard_map.305.refs_0_), channel_id=1, source_target_pairs={{0,8},{8,0},{1,9},{9,1},{2,10},{10,2},{3,11},{11,3},{4,12},{12,4},... | collective-permute-start | bytes 2162696 | tf_op jit(solution)/shard_map/ppermute | solution.py:623
  51.4 23.3 %collective-permute-start.8 = (bf16[512,512]{1,0:T(8,128)(2,1)S(1)}, bf16[512,512]{1,0:T(8,128)(2,1)S(1)}, u32[]{:S(2)}, u32[]{:S(2)}) collective-permute-start(bf16[512,512]{1,0:T(8,128)(2,1)S(1)} %bitcast.284), channel_id=1, source_target_pairs={{0,16},{16,0},{1,17},{17,1},{2,18},{18,2},{3,19},{19,3},{4,20},{20... | collective-permute-start | bytes 1572872 | tf_op jit(solution)/shard_map/ppermute | solution.py:623
  54.4 25.5 %collective-permute-start.4 = (bf16[176,2048]{1,0:T(8,128)(2,1)S(1)}, bf16[176,2048]{1,0:T(8,128)(2,1)}, u32[]{:S(2)}, u32[]{:S(2)}) collective-permute-start(bf16[176,2048]{1,0:T(8,128)(2,1)S(1)} %copy-done.14), channel_id=1, source_target_pairs={{0,2},{2,0},{1,3},{3,1},{4,6},{6,4},{5,7},{7,5},{8,10},{10,8},{9,1... | collective-permute-start | bytes 2162696 | tf_op jit(solution)/shard_map/ppermute | solution.py:623
  107.2 257.0 %reduce-scatter.3.cloned.1.call-start = ((), (), s32[]{:S(2)}) async-start(), calls=%async_computation.7 | async-start | bytes 4718592 | tf_op jit(solution)/shard_map/reduce_scatter | solution.py:1153
  138.6 32.4 %collective-permute-start.15 = (bf16[2,2,144,512]{3,2,1,0:T(8,128)(2,1)}, bf16[2,2,144,512]{3,2,1,0:T(8,128)(2,1)}, u32[]{:S(2)}, u32[]{:S(2)}) collective-permute-start(bf16[2,2,144,512]{3,2,1,0:T(8,128)(2,1)} %bitcast.58), channel_id=1, source_target_pairs={{0,4},{4,0},{1,5},{5,1},{2,6},{6,2},{3,7},{7,3},{8,12},{12,8},{9,1... | collective-permute-start | bytes 1769480 | tf_op jit(solution)/shard_map/ppermute | solution.py:597
  142.4 24.0 %collective-permute-start.16 = (bf16[512,512]{1,0:T(8,128)(2,1)}, bf16[512,512]{1,0:T(8,128)(2,1)}, u32[]{:S(2)}, u32[]{:S(2)}) collective-permute-start(bf16[512,512]{1,0:T(8,128)(2,1)} %shard_map.310.refs_0_), channel_id=1, source_target_pairs={{0,4},{4,0},{1,5},{5,1},{2,6},{6,2},{3,7},{7,3},{8,12},{12,8},{9,1... | collective-permute-start | bytes 1572872 | tf_op jit(solution)/shard_map/ppermute | solution.py:623
  142.4 26.4 %collective-permute-start.17 = (bf16[512,512]{1,0:T(8,128)(2,1)}, bf16[512,512]{1,0:T(8,128)(2,1)}, u32[]{:S(2)}, u32[]{:S(2)}) collective-permute-start(bf16[512,512]{1,0:T(8,128)(2,1)} %shard_map.310.refs_0_), channel_id=1, source_target_pairs={{0,16},{16,0},{1,17},{17,1},{2,18},{18,2},{3,19},{19,3},{4,20},{20... | collective-permute-start | bytes 1572872 | tf_op jit(solution)/shard_map/ppermute | solution.py:623
  168.8 24.7 %collective-permute-start.21 = (bf16[128,2048]{1,0:T(8,128)(2,1)}, bf16[128,2048]{1,0:T(8,128)(2,1)}, u32[]{:S(2)}, u32[]{:S(2)}) collective-permute-start(bf16[128,2048]{1,0:T(8,128)(2,1)} %shard_map.312.refs_4_), channel_id=1, source_target_pairs={{0,16},{16,0},{1,17},{17,1},{2,18},{18,2},{3,19},{19,3},{4,20},{20... | collective-permute-start | bytes 1572872 | tf_op jit(solution)/shard_map/ppermute | solution.py:623
  182.2 26.6 %collective-permute-start.20 = (bf16[128,2048]{1,0:T(8,128)(2,1)}, bf16[128,2048]{1,0:T(8,128)(2,1)S(1)}, u32[]{:S(2)}, u32[]{:S(2)}) collective-permute-start(bf16[128,2048]{1,0:T(8,128)(2,1)} %shard_map.312.refs_4_), channel_id=1, source_target_pairs={{0,4},{4,0},{1,5},{5,1},{2,6},{6,2},{3,7},{7,3},{8,12},{12,8},{9,1... | collective-permute-start | bytes 1572872 | tf_op jit(solution)/shard_map/ppermute | solution.py:623
  182.9 25.9 %collective-permute-start.19 = (bf16[512,512]{1,0:T(8,128)(2,1)}, bf16[512,512]{1,0:T(8,128)(2,1)S(1)}, u32[]{:S(2)}, u32[]{:S(2)}) collective-permute-start(bf16[512,512]{1,0:T(8,128)(2,1)} %collective-permute-done.17.refs_2_), channel_id=1, source_target_pairs={{0,4},{4,0},{1,5},{5,1},{2,6},{6,2},{3,7},{7,3},{8,12},{12,8},{9,1... | collective-permute-start | bytes 1572872 | tf_op jit(solution)/shard_map/ppermute | solution.py:623
  193.5 24.6 %collective-permute-start.22 = (bf16[128,2048]{1,0:T(8,128)(2,1)}, bf16[128,2048]{1,0:T(8,128)(2,1)S(1)}, u32[]{:S(2)}, u32[]{:S(2)}) collective-permute-start(bf16[128,2048]{1,0:T(8,128)(2,1)} %collective-permute-done.21.refs_6_), channel_id=1, source_target_pairs={{0,4},{4,0},{1,5},{5,1},{2,6},{6,2},{3,7},{7,3},{8,12},{12,8},{9,1... | collective-permute-start | bytes 1572872 | tf_op jit(solution)/shard_map/ppermute | solution.py:623
  283.2 24.7 %collective-permute-start.25 = (bf16[2,128,2048]{2,1,0:T(8,128)(2,1)S(1)}, bf16[2,128,2048]{2,1,0:T(8,128)(2,1)S(1)}, u32[]{:S(2)}, u32[]{:S(2)}) collective-permute-start(bf16[2,128,2048]{2,1,0:T(8,128)(2,1)S(1)} %dynamic-slice_bitcast_fusion.2), channel_id=1, source_target_pairs={{0,4},{4,0},{1,5},{5,1},{2,6},{6,2},{3,7},{7,3},{8,12},{12,8},{9,1... | collective-permute-start | bytes 3145736 | tf_op jit(solution)/shard_map/ppermute | solution.py:623
  287.1 22.5 %collective-permute-start.24 = (bf16[2,128,512]{2,1,0:T(8,128)(2,1)S(1)}, bf16[2,128,512]{2,1,0:T(8,128)(2,1)S(1)}, u32[]{:S(2)}, u32[]{:S(2)}) collective-permute-start(bf16[2,128,512]{2,1,0:T(8,128)(2,1)S(1)} %fusion.20), channel_id=1, source_target_pairs={{16,0},{17,1},{18,2},{19,3},{20,4},{21,5},{22,6},{23,7},{24,8},{25... | collective-permute-start | bytes 786440 | tf_op jit(solution)/shard_map/ppermute | solution.py:615
  313.0 187.1 %reduce-scatter.5.cloned.1.call-start = ((), (), s32[]{:S(2)}) async-start(), calls=%async_computation.8 | async-start | bytes 4718592 | tf_op jit(solution)/shard_map/reduce_scatter | solution.py:1212
  314.6 26.4 %collective-permute-start.26 = (bf16[2,2,256,512]{3,2,1,0:T(8,128)(2,1)S(1)}, bf16[2,2,256,512]{3,2,1,0:T(8,128)(2,1)S(1)}, u32[]{:S(2)}, u32[]{:S(2)}) collective-permute-start(bf16[2,2,256,512]{3,2,1,0:T(8,128)(2,1)S(1)} %dynamic-slice_bitcast_fusion.1), channel_id=1, source_target_pairs={{0,4},{4,0},{1,5},{5,1},{2,6},{6,2},{3,7},{7,3},{8,12},{12,8},{9,1... | collective-permute-start | bytes 3145736 | tf_op jit(solution)/shard_map/ppermute | solution.py:623
  317.3 25.4 %collective-permute-start.27 = (bf16[128,2048]{1,0:T(8,128)(2,1)S(1)}, bf16[128,2048]{1,0:T(8,128)(2,1)S(1)}, u32[]{:S(2)}, u32[]{:S(2)}) collective-permute-start(bf16[128,2048]{1,0:T(8,128)(2,1)S(1)} %fusion.17), channel_id=1, source_target_pairs={{0,16},{16,0},{1,17},{17,1},{2,18},{18,2},{3,19},{19,3},{4,20},{20... | collective-permute-start | bytes 1572872 | tf_op jit(solution)/shard_map/ppermute | solution.py:623
  380.7 43.8 %all-to-all-start.2 = ((bf16[8,4,64,384]{3,2,1,0:T(8,128)(2,1)}), bf16[8,4,64,384]{3,2,1,0:T(8,128)(2,1)}, u32[]{:S(2)}, u32[]{:S(2)}) async-start(bf16[8,4,64,384]{3,2,1,0:T(8,128)(2,1)} %bitcast.308), calls=%async_computation.4 | async-start | bytes 3145728 | tf_op jit(solution)/shard_map/all_to_all | solution.py:772
  386.7 37.0 %collective-permute-start.34 = (bf16[2,256,512]{2,1,0:T(8,128)(2,1)}, bf16[2,256,512]{2,1,0:T(8,128)(2,1)S(1)}, u32[]{:S(2)}, u32[]{:S(2)}) collective-permute-start(bf16[2,256,512]{2,1,0:T(8,128)(2,1)} %fusion.19), channel_id=1, source_target_pairs={{0,16},{16,0},{1,17},{17,1},{2,18},{18,2},{3,19},{19,3},{4,20},{20... | collective-permute-start | bytes 1572872 | tf_op jit(solution)/shard_map/ppermute | solution.py:623
  394.4 39.6 %collective-permute-start.30 = (bf16[2,2,256,512]{3,2,1,0:T(8,128)(2,1)}, bf16[2,2,256,512]{3,2,1,0:T(8,128)(2,1)}, u32[]{:S(2)}, u32[]{:S(2)}) collective-permute-start(bf16[2,2,256,512]{3,2,1,0:T(8,128)(2,1)} %dynamic-slice_bitcast_fusion), channel_id=1, source_target_pairs={{0,4},{4,0},{1,5},{5,1},{2,6},{6,2},{3,7},{7,3},{8,12},{12,8},{9,1... | collective-permute-start | bytes 3145736 | tf_op jit(solution)/shard_map/ppermute | solution.py:623
  424.6 22.0 %all-to-all-start.3 = ((bf16[8,64,512]{2,1,0:T(8,128)(2,1)}), bf16[8,64,512]{2,1,0:T(8,128)(2,1)S(1)}, u32[]{:S(2)}, u32[]{:S(2)}) async-start(bf16[8,64,512]{2,1,0:T(8,128)(2,1)} %bitcast.120), calls=%async_computation.5 | async-start | bytes 1048576 | tf_op jit(solution)/shard_map/all_to_all | solution.py:1169
  442.4 30.0 %collective-permute-start.31 = (bf16[2,256,512]{2,1,0:T(8,128)(2,1)}, bf16[2,256,512]{2,1,0:T(8,128)(2,1)}, u32[]{:S(2)}, u32[]{:S(2)}) collective-permute-start(bf16[2,256,512]{2,1,0:T(8,128)(2,1)} %fusion.18), channel_id=1, source_target_pairs={{0,16},{16,0},{1,17},{17,1},{2,18},{18,2},{3,19},{19,3},{4,20},{20... | collective-permute-start | bytes 1572872 | tf_op jit(solution)/shard_map/ppermute | solution.py:623
  446.6 27.8 %all-to-all-start.4 = ((f32[32,8,128]{2,1,0:T(8,128)}), f32[32,8,128]{2,1,0:T(8,128)S(1)}, u32[]{:S(2)}, u32[]{:S(2)}) async-start(f32[32,8,128]{2,1,0:T(8,128)} %bitcast.155), calls=%async_computation.6 | async-start | bytes 262144 | tf_op jit(solution)/shard_map/all_to_all | solution.py:1245
  451.3 36.1 %collective-permute-start.33 = (bf16[64,384]{1,0:T(8,128)(2,1)S(1)}, bf16[64,384]{1,0:T(8,128)(2,1)}, u32[]{:S(2)}, u32[]{:S(2)}) collective-permute-start(bf16[64,384]{1,0:T(8,128)(2,1)S(1)} %fusion.29), channel_id=1, source_target_pairs={{0,16},{16,0},{1,17},{17,1},{2,18},{18,2},{3,19},{19,3},{4,20},{20... | collective-permute-start | bytes 147464 | tf_op jit(solution)/shard_map/ppermute | solution.py:623
  (119 other events, 889.1 us)
Sparse Core Ops, SparseCore 0:
  107.3 29.6 all-gather.2
  313.1 48.1 reduce-scatter.2
  378.1 71.8 reduce-scatter.4
